TPU v7x, 32 devices: a whole 2x2x4 slice. The times are simulated.
32 devices in a mesh: wide: 8 (over y, x, core), narrow: 4 (over z).
Axes of the slice: x: 2, y: 2, z: 4, core: 2. Of those that a mesh axis runs over, the one named last changes fastest.
Arguments:
- saturation: float32 [128, 64, 512], P('wide', None, 'narrow'), may hold values from 0.05 to 0.95
- pressure: float32 [128, 64, 512], P('wide', None, 'narrow'), may hold values from -6 to 6
- rock_class: int32 [128, 64, 512], P('wide', None, 'narrow'), may hold values from 0 to 15
- rock_table: float32 [3, 16], replicated, may hold values from 0.2 to 5
- well_columns: int32 [64], replicated, may hold values from 0 to 32767
- well_rates: float32 [64], replicated, may hold values from 2 to 8
- residual: float32 [128, 64, 512], P(None, 'wide', 'narrow'), may hold values from -7 to 7
Outputs:
- sat_new: float32 [128, 64, 512], P('wide', None, 'narrow')
- precond: float32 [128, 64, 512], P(None, 'wide', 'narrow')
Inputs may be any that keep to these rules, and one draw needn't show every extreme that they name: `well_columns`: a well with column c injects into every depth layer at row c // 512, column c % 512; columns may repeat.
All inputs are finite; a program needn't handle non-finite values.
Results may differ from a plain program's by a relative error of at most 0.0003.
Values sent between devices are 32-bit elements; how exact they have to be, the bound alone decides.
A program may use at most 64 MiB of HBM per device.

v0:
```python
import jax
import jax.numpy as jnp
from jax import lax
from jax.sharding import PartitionSpec as P

SWEEPS = 6


compress = 0.05
relax = 0.8
gravity = 0.5
courant = 0.5
tiny = 1e-06


def extended_2(block, sides, width):
    for axis, dim in sides:
        count = lax.axis_size(axis)
        forward = [(i, i + 1) for i in range(count - 1)]
        backward = [(target, source) for source, target in forward]
        low = lax.ppermute(
            lax.slice_in_dim(block, block.shape[dim] - width, None, axis=dim), axis, forward
        )
        high = lax.ppermute(lax.slice_in_dim(block, 0, width, axis=dim), axis, backward)
        block = jnp.concatenate([low, block, high], axis=dim)
    return block


def harmonic(lower_side, upper_side):
    return 2.0 * lower_side * upper_side / (lower_side + upper_side)


def pad_along(array_in, direction):
    widths = [(0, 0)] * array_in.ndim
    widths[direction] = (1, 1)
    return jnp.pad(array_in, widths)


def flows_between(lower_side, upper_side, lift):
    transmit = harmonic(lower_side[1], upper_side[1])
    total_flow = transmit * (lower_side[0] - upper_side[0] + lift)
    water_flow = total_flow * jnp.where(total_flow > 0, lower_side[2], upper_side[2])
    return (total_flow, water_flow)


def local_apply(values, diag_local, depth_inner, row_inner, col_inner):
    depth_pad = pad_along(values, 0)
    row_pad = pad_along(values, 1)
    col_pad = pad_along(values, 2)
    return diag_local * values - (
        depth_inner[:-1] * depth_pad[:-2]
        + depth_inner[1:] * depth_pad[2:]
        + row_inner[:, :-1] * row_pad[:, :-2]
        + row_inner[:, 1:] * row_pad[:, 2:]
        + col_inner[:, :, :-1] * col_pad[:, :, :-2]
        + col_inner[:, :, 1:] * col_pad[:, :, 2:]
    )


def coarse_solve(rows, column_count):
    rhs_total = rows[:, 0]
    diagonal = rows[:, 1]
    low_rows = rows[:, 2]
    high_rows = rows[:, 3]
    low_cols = rows[:, 4]
    high_cols = rows[:, 5]
    matrix = (
        jnp.diag(diagonal)
        - jnp.diag(low_rows[column_count:], -column_count)
        - jnp.diag(high_rows[:-column_count], column_count)
        - jnp.diag(low_cols[1:], -1)
        - jnp.diag(high_cols[:-1], 1)
    )
    factor = jnp.linalg.cholesky(matrix)
    return jax.scipy.linalg.cho_solve((factor, True), rhs_total)


def rock_lookup(rock_class, rock_table):
    perm_cell = jnp.zeros(rock_class.shape, jnp.float32)
    water_gain = jnp.zeros(rock_class.shape, jnp.float32)
    oil_gain = jnp.zeros(rock_class.shape, jnp.float32)
    for number in range(rock_table.shape[1]):
        matched = rock_class == number
        perm_cell = jnp.where(matched, rock_table[0, number], perm_cell)
        water_gain = jnp.where(matched, rock_table[1, number], water_gain)
        oil_gain = jnp.where(matched, rock_table[2, number], oil_gain)
    return (perm_cell, water_gain, oil_gain)


def coarse_correction(cell_coeff, row_faces, col_faces, residual, narrow_count):
    low_rows = jnp.sum(row_faces[:, 0])
    high_rows = jnp.sum(row_faces[:, -1])
    low_cols = jnp.sum(col_faces[:, :, 0])
    high_cols = jnp.sum(col_faces[:, :, -1])
    diagonal = compress * jnp.sum(cell_coeff) + low_rows + high_rows + low_cols + high_cols
    own_row = jnp.stack([jnp.sum(residual), diagonal, low_rows, high_rows, low_cols, high_cols])[
        None
    ]
    rows = lax.all_gather(own_row, ("wide", "narrow"), axis=0, tiled=True)
    solved = coarse_solve(rows, narrow_count)
    place = lax.axis_index("wide") * narrow_count + lax.axis_index("narrow")
    return lax.dynamic_index_in_dim(solved, place, 0, keepdims=False)


def relax_and_average(
    residual, cell_coeff, coeff_ext, diag_local, depth_inner, row_inner, col_inner
):
    values = relax * residual / diag_local
    for number in range(SWEEPS - 1):
        values = (
            values
            + relax
            * (residual - local_apply(values, diag_local, depth_inner, row_inner, col_inner))
            / diag_local
        )
    values_ext = extended_2(values, (("wide", 1), ("narrow", 2)), 1)
    weighted = cell_coeff * values
    weights = cell_coeff
    weighted = weighted.at[:, 0, :].add(coeff_ext[:, 0, 1:-1] * values_ext[:, 0, 1:-1])
    weights = weights.at[:, 0, :].add(coeff_ext[:, 0, 1:-1])
    weighted = weighted.at[:, -1, :].add(coeff_ext[:, -1, 1:-1] * values_ext[:, -1, 1:-1])
    weights = weights.at[:, -1, :].add(coeff_ext[:, -1, 1:-1])
    weighted = weighted.at[:, :, 0].add(coeff_ext[:, 1:-1, 0] * values_ext[:, 1:-1, 0])
    weights = weights.at[:, :, 0].add(coeff_ext[:, 1:-1, 0])
    weighted = weighted.at[:, :, -1].add(coeff_ext[:, 1:-1, -1] * values_ext[:, 1:-1, -1])
    weights = weights.at[:, :, -1].add(coeff_ext[:, 1:-1, -1])
    return weighted / weights


def shards(saturation, pressure, rock_class, rock_table, well_columns, well_rates, residual):
    slab_depth, rows_all, cols_dev = saturation.shape
    wide_count = lax.axis_size("wide")
    narrow_count = lax.axis_size("narrow")
    perm_cell, water_gain, oil_gain = rock_lookup(rock_class, rock_table)
    water_mob = water_gain * saturation * saturation
    oil_mob = oil_gain * (1.0 - saturation) * (1.0 - saturation)
    water_frac = water_mob / (water_mob + oil_mob)
    stacked = jnp.stack([pressure, perm_cell, water_frac])
    extended = extended_2(stacked, (("wide", 1), ("narrow", 3)), 1)
    centre = extended[:, 1:-1, :, 1:-1]
    depth_total, depth_water = flows_between(
        extended[:, :-1, :, 1:-1], extended[:, 1:, :, 1:-1], gravity
    )
    row_padded = jnp.pad(centre, ((0, 0), (0, 0), (1, 1), (0, 0)))
    row_total, row_water = flows_between(row_padded[:, :, :-1], row_padded[:, :, 1:], 0.0)
    col_total, col_water = flows_between(extended[:, 1:-1, :, :-1], extended[:, 1:-1, :, 1:], 0.0)
    net_water = (
        depth_water[1:]
        - depth_water[:-1]
        + (row_water[:, 1:] - row_water[:, :-1])
        + (col_water[:, :, 1:] - col_water[:, :, :-1])
    )
    outflow = (
        jnp.maximum(depth_total[1:], 0.0)
        + jnp.maximum(-depth_total[:-1], 0.0)
        + (jnp.maximum(row_total[:, 1:], 0.0) + jnp.maximum(-row_total[:, :-1], 0.0))
        + (jnp.maximum(col_total[:, :, 1:], 0.0) + jnp.maximum(-col_total[:, :, :-1], 0.0))
    )
    top_rate = lax.pmax(jnp.max(outflow), ("wide", "narrow"))
    step_size = courant / (top_rate + tiny)
    global_cols = cols_dev * narrow_count
    column_start = lax.axis_index("narrow") * cols_dev
    well_row = well_columns // global_cols
    well_col = well_columns % global_cols - column_start
    inside = (well_col >= 0) & (well_col < cols_dev)
    target = jnp.where(inside, well_row * cols_dev + well_col, rows_all * cols_dev)
    source = jnp.zeros((rows_all * cols_dev,), jnp.float32).at[target].add(well_rates, mode="drop")
    source = source.reshape(rows_all, cols_dev)
    sat_new = saturation - step_size * net_water + step_size * source[None]
    coefficient = perm_cell * (
        water_gain * sat_new * sat_new + oil_gain * (1.0 - sat_new) * (1.0 - sat_new)
    )
    blocks = coefficient.reshape(slab_depth, wide_count, rows_all // wide_count, cols_dev)
    zero_row = jnp.zeros((slab_depth, 1, 1, cols_dev), jnp.float32)
    lower_rim = jnp.concatenate([zero_row, blocks[:, :-1, -1:, :]], axis=1)
    upper_rim = jnp.concatenate([blocks[:, 1:, :1, :], zero_row], axis=1)
    framed = jnp.concatenate([lower_rim, blocks, upper_rim], axis=2)
    moved = lax.all_to_all(framed, "wide", split_axis=1, concat_axis=0, tiled=True)
    rimmed = moved.reshape(moved.shape[0], moved.shape[2], cols_dev)
    coeff_ext = extended_2(rimmed, (("narrow", 2),), 1)
    cell_coeff = coeff_ext[:, 1:-1, 1:-1]
    depth_faces = harmonic(cell_coeff[:-1], cell_coeff[1:])
    row_faces = harmonic(coeff_ext[:, :-1, 1:-1], coeff_ext[:, 1:, 1:-1])
    col_faces = harmonic(coeff_ext[:, 1:-1, :-1], coeff_ext[:, 1:-1, 1:])
    depth_inner = pad_along(depth_faces, 0)
    row_inner = pad_along(row_faces[:, 1:-1], 1)
    col_inner = pad_along(col_faces[:, :, 1:-1], 2)
    diag_local = (
        compress * cell_coeff
        + depth_inner[:-1]
        + depth_inner[1:]
        + row_inner[:, :-1]
        + row_inner[:, 1:]
        + col_inner[:, :, :-1]
        + col_inner[:, :, 1:]
    )
    averaged = relax_and_average(
        residual, cell_coeff, coeff_ext, diag_local, depth_inner, row_inner, col_inner
    )
    coarse_value = coarse_correction(cell_coeff, row_faces, col_faces, residual, narrow_count)
    precond = averaged + coarse_value
    return (sat_new, precond)


def solution(mesh):
    placed = (
        P("wide", None, "narrow"),
        P("wide", None, "narrow"),
        P("wide", None, "narrow"),
        P(),
        P(),
        P(),
        P(None, "wide", "narrow"),
    )
    return jax.shard_map(
        shards,
        mesh=mesh,
        in_specs=placed,
        out_specs=(P("wide", None, "narrow"), P(None, "wide", "narrow")),
        check_vma=False,
    )
```

profile of v0, /device:TPU:1, one launch (start us, length us, event | category | flops | bytes accessed | tf_op | source)
XLA Modules:
  0.0 236.0 jit_solution(9624230702709681645)
XLA Ops:
  0.6 1.7 fusion.144
  2.4 2.1 fusion.142
  4.5 2.1 fusion.143
  6.6 12.7 %select_select_fusion.2 = (f32[16,64,128]{2,1,0:T(8,128)S(1)}, pred[16,64,128]{2,1,0:T(8,128)(4,1)S(1)}, pred[16,64,128]{2,1,0:T(8,128)(4,1)S(1)}, pred[16,64,12...) fusion(f32[]{:T(128)} %bitcast.16, f32[]{:T(128)} %bitcast.15, ...), kind=kLoop, calls=%fused_computation.217 | loop fusion | flops 4194304 | bytes 3145792 | tf_op jit(solution)/shard_map/jit(_where)/select_n | solution.py:84
  19.3 22.3 %fusion.90 = (f32[1,16,64,128]{3,2,1,0:T(8,128)S(1)}, f32[16,64,128]{2,1,0:T(8,128)}, f32[16,64,128]{2,1,0:T(8,128)}) fusion(f32[16,64,128]{2,1,0:T(8,128)S(1)} %copy-done.8, pred[16,64,128]{2,1,0:T(8,128)(4,1)S(1)} %get-tuple-element.140, pred[16,64,128]{2,1,0:T(8,128)(4,1)S(1)} %get-tuple-element.139, pred[16,64,128]{2,1,0:T(8,128)(4,1)S(1)} %get-tuple-element.138, ...), kind=kLoop, calls=%fused_computation.171 | loop fusion | flops 5111808 | bytes 4194432 | tf_op jit(solution)/shard_map/stack | solution.py:138
  41.8 4.5 %collective-permute-start = (f32[3,1,64,128]{3,2,1,0:T(8,128)S(1)}, f32[3,1,64,128]{3,2,1,0:T(8,128)S(1)}, u32[]{:S(2)}, u32[]{:S(2)}) collective-permute-start(f32[3,1,64,128]{3,2,1,0:T(8,128)S(1)} %get-tuple-element.148), channel_id=1, source_target_pairs={{0,4},{4,8},{8,12},{12,16},{16,20},{20,24},{24,28},{1,5},{5,9},{9,... | collective-permute-start | bytes 294920 | tf_op jit(solution)/shard_map/ppermute | solution.py:21
  46.3 1.9 collective-permute-start.1
  49.6 2.7 %collective-permute-done.1 = f32[3,1,64,128]{3,2,1,0:T(8,128)S(1)} collective-permute-done((f32[3,1,64,128]{3,2,1,0:T(8,128)S(1)}, f32[3,1,64,128]{3,2,1,0:T(8,128)S(1)}, u32[]{:S(2)}, u32[]{:S(2)}) %collective-permute-start.1) | collective-permute-done | bytes 98336 | tf_op jit(solution)/shard_map/ppermute | solution.py:24
  52.4 1.9 fusion.136
  54.3 2.7 %copy.87 = f32[3,18,64,1]{2,3,1,0:T(1,128)} copy(f32[3,18,64,1]{3,2,1,0:T(8,128)} %get-tuple-element.144) | data formatting | bytes 27648 | tf_op jit(solution)/shard_map/slice | solution.py:22
  59.4 4.6 %collective-permute-start.2 = (f32[3,18,64,1]{2,3,1,0:T(1,128)}, f32[3,18,64,1]{2,3,1,0:T(1,128)}, u32[]{:S(2)}, u32[]{:S(2)}) collective-permute-start(f32[3,18,64,1]{2,3,1,0:T(1,128)} %copy.87), channel_id=1, source_target_pairs={{0,1},{1,2},{2,3},{4,5},{5,6},{6,7},{8,9},{9,10},{10,11},{12,13},{... | collective-permute-start | bytes 41480 | tf_op jit(solution)/shard_map/ppermute | solution.py:21
  67.2 2.5 %copy.90 = f32[3,18,64,1]{3,2,1,0:T(8,128)} copy(f32[3,18,64,1]{2,3,1,0:T(1,128)} %collective-permute-done.3) | data formatting | bytes 27648 | tf_op jit(solution)/shard_map/ppermute | solution.py:24
  69.8 2.2 fusion.5
  73.0 1.6 scatter_custom_fusion
  74.6 39.3 %pmax.7 = f32[]{:T(128)} all-reduce(f32[]{:T(128)} %fusion.112), channel_id=1, replica_groups=mesh['wide'=8,'narrow'=4] {'wide','narrow'}, use_global_device_ids=true, to_apply=%region_1.2 | all-reduce | flops 1 | bytes 8 | tf_op jit(solution)/shard_map/pmax | solution.py:159
  115.4 2.8 %fusion.2 = f32[16,64,129]{2,1,0:T(8,128)S(1)} fusion(f32[3,18,64,1]{3,2,1,0:T(8,128)} %copy.90, f32[3,1,64,128]{3,2,1,0:T(8,128)S(1)} %collective-permute-done.1, f32[3,1,64,128]{3,2,1,0:T(8,128)S(1)} %collective-permute-done, f32[1,16,64,128]{3,2,1,0:T(8,128)S(1)} %get-tuple-element.141, f32[1,16,64,128]{3,2,1,0:T(8,128)S(1)} %bitcast.176, ...), kind=kLoop, calls=%fused_computation.34 | loop fusion | flops 5151744 | bytes 2325504 | tf_op jit(solution)/shard_map/mul | solution.py:42
  121.1 5.5 %all-to-all-start = ((f32[16,8,10,128]{3,0,2,1:T(8,128)}), f32[16,8,10,128]{3,0,2,1:T(8,128)S(1)}, u32[]{:S(2)}, u32[]{:S(2)}) async-start(f32[16,8,10,128]{3,0,2,1:T(8,128)} %copy.91), calls=%async_computation | async-start | bytes 1310720 | tf_op jit(solution)/shard_map/all_to_all | solution.py:178
  127.5 6.9 %all-to-all-done = f32[16,8,10,128]{3,0,2,1:T(8,128)S(1)} async-done(((f32[16,8,10,128]{3,0,2,1:T(8,128)}), f32[16,8,10,128]{3,0,2,1:T(8,128)S(1)}, u32[]{:S(2)}, u32[]{:S(2)}) %all-to-all-start) | async-done | bytes 655392 | tf_op jit(solution)/shard_map/all_to_all | solution.py:178
  137.7 4.6 %collective-permute-start.4 = (f32[128,10,1]{0,1,2:T(8,128)S(1)}, f32[128,10,1]{0,1,2:T(8,128)S(1)}, u32[]{:S(2)}, u32[]{:S(2)}) collective-permute-start(f32[128,10,1]{0,1,2:T(8,128)S(1)} %copy.94), channel_id=1, source_target_pairs={{0,1},{1,2},{2,3},{4,5},{5,6},{6,7},{8,9},{9,10},{10,11},{12,13},{... | collective-permute-start | bytes 15368 | tf_op jit(solution)/shard_map/ppermute | solution.py:21
  142.2 1.6 slice_reduce_fusion.2
  146.7 1.9 fusion.118
  151.7 3.1 %stack.43 = f32[6]{0:T(128)S(1)} concatenate(f32[1]{0:T(128)} %bitcast.73, f32[1]{0:T(128)} %bitcast.74, f32[1]{0:T(128)} %bitcast.75, f32[1]{0:T(128)} %bitcast.76, f32[1]{0:T(128)} %bitcast.77, f32[1]{0:T(128)} %bitcast.78), dimensions={0} | concatenate | bytes 48 | tf_op jit(solution)/shard_map/stack | solution.py:96
  155.1 42.0 %all-reduce.25 = f32[192]{0:T(256)S(1)} all-reduce(f32[192]{0:T(256)S(1)} %dynamic-update-slice.27), channel_id=2, replica_groups=mesh['wide'=8,'narrow'=4] {'wide','narrow'}, use_global_device_ids=true, to_apply=%add.25 | all-reduce | flops 192 | bytes 1536
  197.7 3.5 %fusion.30 = f32[128,8,128]{2,0,1:T(8,128)S(1)} fusion(f32[128,8,128]{2,0,1:T(8,128)} %get-tuple-element.116, f32[128,8,128]{2,0,1:T(8,128)S(1)} %get-tuple-element.117, f32[128,8,128]{2,1,0:T(8,128)S(1)} %copy-done, f32[127,8,128]{2,0,1:T(8,128)S(1)} %add_divide_fusion.3, f32[128,7,128]{2,0,1:T(8,128)S(1)} %slice.920, f32[128,8,127]{2,0,1:T(8,128)S(1)} %slice.923), kind=kLoop, calls=%fused_computation.111 | loop fusion | flops 2752512 | bytes 3596288 | tf_op jit(solution)/shard_map/add | solution.py:111
  203.1 1.6 slice_multiply_fusion.2
  205.0 2.9 %cholesky.16 = f32[32,32]{1,0:T(8,128)S(1)} custom-call(f32[32,32]{1,0:T(8,128)S(1)} %add_multiply_fusion), custom_call_target="Cholesky" | custom-call | tf_op jit(solution)/shard_map/jit(cholesky)/cholesky | solution.py:74
  209.4 2.4 %custom-call.10 = f32[1,32,32]{1,2,0:T(8,128)S(1)} custom-call(f32[1,32,32]{2,1,0:T(8,128)S(1)} %fusion.123), custom_call_target="InvertDiagBlocksLowerTriangular" | custom-call | tf_op jit(solution)/shard_map/jit(_cho_solve)/triangular_solve | solution.py:75
  212.7 3.4 %collective-permute-start.7 = (f32[128,1,128]{2,0,1:T(8,128)S(1)}, f32[128,1,128]{2,0,1:T(8,128)S(1)}, u32[]{:S(2)}, u32[]{:S(2)}) collective-permute-start(f32[128,1,128]{2,0,1:T(8,128)S(1)} %get-tuple-element.160), channel_id=1, source_target_pairs={{4,0},{8,4},{12,8},{16,12},{20,16},{24,20},{28,24},{5,1},{9,5},{13... | collective-permute-start | bytes 196616 | tf_op jit(solution)/shard_map/ppermute | solution.py:24
  216.1 3.8 %collective-permute-start.6 = (f32[128,1,128]{2,0,1:T(8,128)S(1)}, f32[128,1,128]{2,0,1:T(8,128)S(1)}, u32[]{:S(2)}, u32[]{:S(2)}) collective-permute-start(f32[128,1,128]{2,0,1:T(8,128)S(1)} %get-tuple-element.161), channel_id=1, source_target_pairs={{0,4},{4,8},{8,12},{12,16},{16,20},{20,24},{24,28},{1,5},{5,9},{9,... | collective-permute-start | bytes 196616 | tf_op jit(solution)/shard_map/ppermute | solution.py:21
  222.9 2.4 %collective-permute-start.8 = (f32[128,10,1]{0,1,2:T(8,128)S(1)}, f32[128,10,1]{0,1,2:T(8,128)S(1)}, u32[]{:S(2)}, u32[]{:S(2)}) collective-permute-start(f32[128,10,1]{0,1,2:T(8,128)S(1)} %copy.103), channel_id=1, source_target_pairs={{0,1},{1,2},{2,3},{4,5},{5,6},{6,7},{8,9},{9,10},{10,11},{12,13},{... | collective-permute-start | bytes 15368 | tf_op jit(solution)/shard_map/ppermute | solution.py:21
  231.1 1.5 scatter-add.55
  232.6 1.5 scatter-add.40
  (111 shorter events, 34.7 us)
Async XLA Ops:
  6.6 12.7 %copy-start.8 = (f32[16,64,128]{2,1,0:T(8,128)S(1)}, f32[16,64,128]{2,1,0:T(8,128)}, u32[]{:S(2)}) copy-start(f32[16,64,128]{2,1,0:T(8,128)} %param.23) | copy-start | bytes 1572868
  19.3 22.3 %copy-start.1 = (f32[16,64,128]{2,1,0:T(8,128)S(1)}, f32[16,64,128]{2,1,0:T(8,128)}, u32[]{:S(2)}) copy-start(f32[16,64,128]{2,1,0:T(8,128)} %param.24) | copy-start | bytes 1572868
  41.6 6.7 %copy-start.12 = (s32[64]{0:T(128)S(1)}, s32[64]{0:T(128)}, u32[]{:S(2)}) copy-start(s32[64]{0:T(128)} %param.27) | copy-start | bytes 772
  41.8 7.8 %collective-permute-start = (f32[3,1,64,128]{3,2,1,0:T(8,128)S(1)}, f32[3,1,64,128]{3,2,1,0:T(8,128)S(1)}, u32[]{:S(2)}, u32[]{:S(2)}) collective-permute-start(f32[3,1,64,128]{3,2,1,0:T(8,128)S(1)} %get-tuple-element.148), channel_id=1, source_target_pairs={{0,4},{4,8},{8,12},{12,16},{16,20},{20,24},{24,28},{1,5},{5,9},{9,... | collective-permute-start | bytes 294920 | tf_op jit(solution)/shard_map/ppermute | solution.py:21
  46.3 5.9 %collective-permute-start.1 = (f32[3,1,64,128]{3,2,1,0:T(8,128)S(1)}, f32[3,1,64,128]{3,2,1,0:T(8,128)S(1)}, u32[]{:S(2)}, u32[]{:S(2)}) collective-permute-start(f32[3,1,64,128]{3,2,1,0:T(8,128)S(1)} %get-tuple-element.149), channel_id=1, source_target_pairs={{4,0},{8,4},{12,8},{16,12},{20,16},{24,20},{28,24},{5,1},{9,5},{13... | collective-permute-start | bytes 294920 | tf_op jit(solution)/shard_map/ppermute | solution.py:24
  58.1 9.1 %collective-permute-start.3 = (f32[3,18,64,1]{2,3,1,0:T(1,128)}, f32[3,18,64,1]{2,3,1,0:T(1,128)}, u32[]{:S(2)}, u32[]{:S(2)}) collective-permute-start(f32[3,18,64,1]{2,3,1,0:T(1,128)} %copy.89), channel_id=1, source_target_pairs={{1,0},{2,1},{3,2},{5,4},{6,5},{7,6},{9,8},{10,9},{11,10},{13,12},{... | collective-permute-start | bytes 41480 | tf_op jit(solution)/shard_map/ppermute | solution.py:24
  59.4 6.5 %collective-permute-start.2 = (f32[3,18,64,1]{2,3,1,0:T(1,128)}, f32[3,18,64,1]{2,3,1,0:T(1,128)}, u32[]{:S(2)}, u32[]{:S(2)}) collective-permute-start(f32[3,18,64,1]{2,3,1,0:T(1,128)} %copy.87), channel_id=1, source_target_pairs={{0,1},{1,2},{2,3},{4,5},{5,6},{6,7},{8,9},{9,10},{10,11},{12,13},{... | collective-permute-start | bytes 41480 | tf_op jit(solution)/shard_map/ppermute | solution.py:21
  69.8 2.2 copy-start.5
  69.8 2.2 copy-start.7
  115.4 2.9 %copy-start.4 = (f32[17,64,128]{2,1,0:T(8,128)S(1)}, f32[17,64,128]{2,1,0:T(8,128)}, u32[]{:S(2)}) copy-start(f32[17,64,128]{2,1,0:T(8,128)} %get-tuple-element.120) | copy-start | bytes 1671172
  115.4 2.9 %copy-start.6 = (f32[16,65,128]{2,1,0:T(8,128)S(1)}, f32[16,65,128]{2,1,0:T(8,128)}, u32[]{:S(2)}) copy-start(f32[16,65,128]{2,1,0:T(8,128)} %get-tuple-element.122) | copy-start | bytes 1597444
  115.4 2.9 %copy-start.9 = (f32[16,64,128]{2,1,0:T(8,128)S(1)}, f32[16,64,128]{2,1,0:T(8,128)}, u32[]{:S(2)}) copy-start(f32[16,64,128]{2,1,0:T(8,128)} %param.23) | copy-start | bytes 1572868
  115.4 2.9 %copy-start.10 = (f32[16,64,128]{2,1,0:T(8,128)S(1)}, f32[16,64,128]{2,1,0:T(8,128)}, u32[]{:S(2)}) copy-start(f32[16,64,128]{2,1,0:T(8,128)} %get-tuple-element.142) | copy-start | bytes 1572868
  115.4 2.9 %copy-start.11 = (f32[16,64,128]{2,1,0:T(8,128)S(1)}, f32[16,64,128]{2,1,0:T(8,128)}, u32[]{:S(2)}) copy-start(f32[16,64,128]{2,1,0:T(8,128)} %get-tuple-element.143) | copy-start | bytes 1572868
  119.9 6.8 %copy-start = (f32[128,8,128]{2,1,0:T(8,128)S(1)}, f32[128,8,128]{2,1,0:T(8,128)}, u32[]{:S(2)}) copy-start(f32[128,8,128]{2,1,0:T(8,128)} %param.29) | copy-start | bytes 1572868
  121.1 13.2 %all-to-all-start = ((f32[16,8,10,128]{3,0,2,1:T(8,128)}), f32[16,8,10,128]{3,0,2,1:T(8,128)S(1)}, u32[]{:S(2)}, u32[]{:S(2)}) async-start(f32[16,8,10,128]{3,0,2,1:T(8,128)} %copy.91), calls=%async_computation | async-start | bytes 1310720 | tf_op jit(solution)/shard_map/all_to_all | solution.py:178
  136.4 8.8 %collective-permute-start.5 = (f32[128,10,1]{0,1,2:T(8,128)S(1)}, f32[128,10,1]{0,1,2:T(8,128)S(1)}, u32[]{:S(2)}, u32[]{:S(2)}) collective-permute-start(f32[128,10,1]{0,1,2:T(8,128)S(1)} %copy.96), channel_id=1, source_target_pairs={{1,0},{2,1},{3,2},{5,4},{6,5},{7,6},{9,8},{10,9},{11,10},{13,12},{... | collective-permute-start | bytes 15368 | tf_op jit(solution)/shard_map/ppermute | solution.py:24
  137.7 7.2 %collective-permute-start.4 = (f32[128,10,1]{0,1,2:T(8,128)S(1)}, f32[128,10,1]{0,1,2:T(8,128)S(1)}, u32[]{:S(2)}, u32[]{:S(2)}) collective-permute-start(f32[128,10,1]{0,1,2:T(8,128)S(1)} %copy.94), channel_id=1, source_target_pairs={{0,1},{1,2},{2,3},{4,5},{5,6},{6,7},{8,9},{9,10},{10,11},{12,13},{... | collective-permute-start | bytes 15368 | tf_op jit(solution)/shard_map/ppermute | solution.py:21
  212.7 8.2 %collective-permute-start.7 = (f32[128,1,128]{2,0,1:T(8,128)S(1)}, f32[128,1,128]{2,0,1:T(8,128)S(1)}, u32[]{:S(2)}, u32[]{:S(2)}) collective-permute-start(f32[128,1,128]{2,0,1:T(8,128)S(1)} %get-tuple-element.160), channel_id=1, source_target_pairs={{4,0},{8,4},{12,8},{16,12},{20,16},{24,20},{28,24},{5,1},{9,5},{13... | collective-permute-start | bytes 196616 | tf_op jit(solution)/shard_map/ppermute | solution.py:24
  216.1 5.1 %collective-permute-start.6 = (f32[128,1,128]{2,0,1:T(8,128)S(1)}, f32[128,1,128]{2,0,1:T(8,128)S(1)}, u32[]{:S(2)}, u32[]{:S(2)}) collective-permute-start(f32[128,1,128]{2,0,1:T(8,128)S(1)} %get-tuple-element.161), channel_id=1, source_target_pairs={{0,4},{4,8},{8,12},{12,16},{16,20},{20,24},{24,28},{1,5},{5,9},{9,... | collective-permute-start | bytes 196616 | tf_op jit(solution)/shard_map/ppermute | solution.py:21
  222.3 3.1 %copy-start.2 = (f32[128,8,128]{2,0,1:T(8,128)S(1)}, f32[128,8,128]{2,0,1:T(8,128)}, u32[]{:S(2)}) copy-start(f32[128,8,128]{2,0,1:T(8,128)} %get-tuple-element.114) | copy-start | bytes 1572868
  222.3 3.0 %copy-start.3 = (f32[128,8,128]{2,0,1:T(8,128)S(1)}, f32[128,8,128]{2,0,1:T(8,128)}, u32[]{:S(2)}) copy-start(f32[128,8,128]{2,0,1:T(8,128)} %get-tuple-element.155) | copy-start | bytes 1572868
  222.9 4.6 %collective-permute-start.8 = (f32[128,10,1]{0,1,2:T(8,128)S(1)}, f32[128,10,1]{0,1,2:T(8,128)S(1)}, u32[]{:S(2)}, u32[]{:S(2)}) collective-permute-start(f32[128,10,1]{0,1,2:T(8,128)S(1)} %copy.103), channel_id=1, source_target_pairs={{0,1},{1,2},{2,3},{4,5},{5,6},{6,7},{8,9},{9,10},{10,11},{12,13},{... | collective-permute-start | bytes 15368 | tf_op jit(solution)/shard_map/ppermute | solution.py:21
  226.2 4.4 %collective-permute-start.9 = (f32[128,10,1]{0,1,2:T(8,128)S(1)}, f32[128,10,1]{0,1,2:T(8,128)S(1)}, u32[]{:S(2)}, u32[]{:S(2)}) collective-permute-start(f32[128,10,1]{0,1,2:T(8,128)S(1)} %copy.106), channel_id=1, source_target_pairs={{1,0},{2,1},{3,2},{5,4},{6,5},{7,6},{9,8},{10,9},{11,10},{13,12},{... | collective-permute-start | bytes 15368 | tf_op jit(solution)/shard_map/ppermute | solution.py:24
where the time goes:
time: 240 us; the launch traced here: 236 us
  blocking collectives  81.3 us (34%)
  other arithmetic  70.7 us (29%)
  starting transfers between devices  34.6 us (14%)
  local copies, waits for them, and re-layouts  33.9 us (14%)
  waiting for transfers between devices  10.2 us (4%)
  between operations  4.98 us (2%)
    unnamed x1, blocking collectives  42 us
    pmax x1, blocking collectives, shards(): top_rate = lax.pmax(jnp.max(outflow), ('wide', 'narrow'))  39.3 us
    another operation x2, other arithmetic, shards(): stacked = jnp.stack([pressure, perm_cell, water_frac])  22.4 us
    ppermute x5, starting transfers between devices, extended_2(): lax.ppermute(lax.slice_in_dim(block, block.shape[dim] - width, None, axis...  19.9 us
    select_n x1, other arithmetic, rock_lookup(): perm_cell = jnp.where(matched, rock_table[0, number], perm_cell)  12.7 us
    ppermute x5, starting transfers between devices, extended_2(): lax.ppermute(lax.slice_in_dim(block, 0, width, axis=dim), axis, backward)  9.18 us
    all_to_all x1, waiting for transfers between devices, shards(): lax.all_to_all(framed, 'wide', split_axis=1, concat_axis=0, tiled=True)  6.88 us
    slice x3, local copies, waits for them, and re-layouts, rock_lookup(): oil_gain = jnp.where(matched, rock_table[2, number], oil_gain)  5.93 us
  transfers between devices with their start and end apart: 11, of which 4 were waited for; matrix products, arithmetic and copies ran while one was open for 5% of the time, Pallas kernels for 0%

commit v1 on v0

v1 whole, which is shorter than its diff:
```python
import functools

import jax
import jax.numpy as jnp
from jax import lax
from jax.experimental import pallas as pl
from jax.experimental.pallas import tpu as pltpu
from jax.sharding import PartitionSpec as P

SWEEPS = 6

compress = 0.05
relax = 0.8
gravity = 0.5
courant = 0.5
tiny = 1e-06

F32 = jnp.float32


def harmonic(a, b):
    return 2.0 * a * b / (a + b)


def flows(low, high, lift):
    total = harmonic(low[1], high[1]) * (low[0] - high[0] + lift)
    return total, total * jnp.where(total > 0, low[2], high[2])


def lookup(bits, table_ref, row, count):
    level = [table_ref[row, i] for i in range(count)]
    for bit in bits:
        level = [jnp.where(bit, level[i + 1], level[i]) for i in range(0, len(level), 2)]
    return level[0]


def kernel(
    n_wide, n_narrow,
    sat_ref, pres_ref, rock_ref, table_ref, wcol_ref, wrate_ref, res_ref,
    satnew_ref, prec_ref,
    fields, gains, net, colpack, colhalo, colflow, source, maxw, maxn,
    slab, coef, dface, rface, cface, scale, first, va, vb,
    rowsend, rowhalo, rowterm, packs, packhalo, packterm, cw, cn, mat, rhs,
    sends, recvs,
):
    depth, rows, cols = sat_ref.shape
    layers, brick_rows, _ = res_ref.shape
    w = lax.axis_index("wide")
    k = lax.axis_index("narrow")
    tiles = layers // cols
    band = depth * brick_rows
    has = {"wide": (w > 0, w < n_wide - 1), "narrow": (k > 0, k < n_narrow - 1)}
    place = {"wide": w, "narrow": k}
    size = {"wide": n_wide, "narrow": n_narrow}
    count = [0]

    def slot():
        count[0] += 1
        return count[0] - 1

    barrier = pltpu.get_barrier_semaphore()
    for axis in ("wide", "narrow"):
        for off in range(1, size[axis]):
            peer = lax.rem(place[axis] + off, size[axis])
            pl.semaphore_signal(
                barrier, inc=1, device_id={axis: peer}, device_id_type=pl.DeviceIdType.MESH
            )

    def remote(src, dst, number, axis, peer):
        return pltpu.make_async_remote_copy(
            src_ref=src, dst_ref=dst, send_sem=sends.at[number], recv_sem=recvs.at[number],
            device_id={axis: peer}, device_id_type=pl.DeviceIdType.MESH,
        )

    def neighbours(axis, low_src, high_src, from_low, from_high):
        down, up = slot(), slot()
        me = place[axis]
        has_low, has_high = has[axis]

        @pl.when(has_low)
        def _():
            remote(low_src, from_high, down, axis, me - 1).start()

        @pl.when(has_high)
        def _():
            remote(high_src, from_low, up, axis, me + 1).start()

        def wait():
            @pl.when(has_low)
            def _():
                remote(low_src, from_high, down, axis, me - 1).wait_send()
                remote(high_src, from_low, up, axis, me - 1).wait_recv()

            @pl.when(has_high)
            def _():
                remote(high_src, from_low, up, axis, me + 1).wait_send()
                remote(low_src, from_high, down, axis, me + 1).wait_recv()

        return wait

    def everyone(axis, src_of, dst_from):
        copies = []
        me = place[axis]
        n = size[axis]
        for off in range(1, n):
            number = slot()
            peer = lax.rem(me + off, n)
            copy = remote(src_of(peer), dst_from(me), number, axis, peer)
            copy.start()
            sender = lax.rem(me + n - off, n)
            copies.append((copy, remote(src_of(peer), dst_from(sender), number, axis, peer)))

        def wait():
            for sent, received in copies:
                sent.wait_send()
                received.wait_recv()

        return wait

    lane = lax.broadcasted_iota(jnp.int32, (rows, cols), 1)
    row = lax.broadcasted_iota(jnp.int32, (rows, cols), 0)
    tlane = lax.broadcasted_iota(jnp.int32, (brick_rows, cols), 1)
    trow = lax.broadcasted_iota(jnp.int32, (brick_rows, cols), 0)
    zero = jnp.zeros((brick_rows, cols), F32)
    one = jnp.ones((brick_rows, cols), F32)

    @pl.when(w == 0)
    def _():
        fields[0] = jnp.ones((3, rows, cols), F32)
        rowhalo[0] = jnp.ones((2, layers, cols), F32)

    @pl.when(w == n_wide - 1)
    def _():
        fields[depth + 1] = jnp.ones((3, rows, cols), F32)
        rowhalo[1] = jnp.ones((2, layers, cols), F32)

    @pl.when(k == 0)
    def _():
        colhalo[0] = jnp.ones((rows, cols), F32)
        packhalo[0] = jnp.ones((2, tiles * brick_rows, cols), F32)

    @pl.when(k == n_narrow - 1)
    def _():
        colhalo[1] = jnp.ones((rows, cols), F32)
        packhalo[1] = jnp.ones((2, tiles * brick_rows, cols), F32)

    coef[pl.ds(layers * brick_rows, brick_rows), :] = one
    va[pl.ds(layers * brick_rows, brick_rows), :] = zero
    vb[pl.ds(layers * brick_rows, brick_rows), :] = zero

    rocks = table_ref.shape[1]

    def derive(d, carry):
        packed_low, packed_high = carry
        rock = rock_ref[d]
        bits = []
        step = 1
        while step < rocks:
            bits.append((rock & step) != 0)
            step *= 2
        perm = lookup(bits, table_ref, 0, rocks)
        water = lookup(bits, table_ref, 1, rocks)
        oil = lookup(bits, table_ref, 2, rocks)
        s = sat_ref[d]
        water_mob = water * s * s
        oil_mob = oil * (1.0 - s) * (1.0 - s)
        frac = water_mob / (water_mob + oil_mob)
        gains[d, 0] = water
        gains[d, 1] = oil
        for f, value in enumerate((pres_ref[d], perm, frac)):
            fields[d + 1, f] = value
            turned = pltpu.roll(value, d + f * depth, 1)
            packed_low = jnp.where(lane == d + f * depth, turned, packed_low)
            packed_high = jnp.where(lane == lax.rem(d + f * depth + cols - 1, cols), turned, packed_high)
        return packed_low, packed_high

    blank = jnp.ones((rows, cols), F32)
    packed_low, packed_high = lax.fori_loop(0, depth, derive, (blank, blank))
    colpack[0] = packed_low
    colpack[1] = pltpu.roll(packed_high, 1, 1)

    pl.semaphore_wait(barrier, n_wide + n_narrow - 2)
    wait_planes = neighbours(
        "wide", fields.at[1], fields.at[depth], fields.at[0], fields.at[depth + 1]
    )
    wait_cols = neighbours(
        "narrow", colpack.at[0], colpack.at[1], colhalo.at[0], colhalo.at[1]
    )

    all_cols = cols * n_narrow

    def well(i, total):
        column = wcol_ref[i]
        inside = column % all_cols - k * cols
        return total + jnp.where(
            (row == column // all_cols) & (lane == inside), wrate_ref[i], 0.0
        )

    source[...] = lax.fori_loop(0, wcol_ref.shape[0], well, jnp.zeros((rows, cols), F32))

    def add_res(z, total):
        return total + res_ref[z]

    res_total = lax.fori_loop(0, layers, add_res, zero)

    wait_cols()

    def unpack(block):
        return [block] + [pltpu.roll(block, cols - f * depth, 1) for f in (1, 2)]

    low_total, low_water = flows(unpack(colhalo[0]), unpack(colpack[0]), 0.0)
    high_total, high_water = flows(unpack(colpack[1]), unpack(colhalo[1]), 0.0)
    has_left, has_right = has["narrow"]
    nothing = jnp.zeros((rows, cols), F32)
    colflow[0] = jnp.where(has_left, low_total, nothing)
    colflow[1] = jnp.where(has_left, low_water, nothing)
    colflow[2] = jnp.where(has_right, high_total, nothing)
    colflow[3] = jnp.where(has_right, high_water, nothing)

    wait_planes()
    has_below, has_above = has["wide"]

    def plane(d):
        return [fields[d, f] for f in range(3)]

    under_total, under_water = flows(plane(0), plane(1), gravity)
    under_total = jnp.where(has_below, under_total, nothing)
    under_water = jnp.where(has_below, under_water, nothing)

    def transport(d, carry):
        below_total, below_water, most = carry
        here = plane(d + 1)
        above_total, above_water = flows(here, plane(d + 2), gravity)
        open_face = (d < depth - 1) | has_above
        above_total = jnp.where(open_face, above_total, nothing)
        above_water = jnp.where(open_face, above_water, nothing)
        flow = above_water - below_water
        out = jnp.maximum(above_total, 0.0) + jnp.maximum(-below_total, 0.0)

        total, water = flows(here, [pltpu.roll(x, rows - 1, 0) for x in here], 0.0)
        total = jnp.where(row == rows - 1, 0.0, total)
        water = jnp.where(row == rows - 1, 0.0, water)
        flow = flow + (water - pltpu.roll(water, 1, 0))
        out = out + (jnp.maximum(total, 0.0) + jnp.maximum(-pltpu.roll(total, 1, 0), 0.0))

        total, water = flows(here, [pltpu.roll(x, cols - 1, 1) for x in here], 0.0)
        to_low = lax.rem(cols - d, cols)
        low = [jnp.where(lane == 0, pltpu.roll(colflow[i], to_low, 1), pltpu.roll(x, 1, 1))
               for i, x in ((0, total), (1, water))]
        high = [jnp.where(lane == cols - 1, pltpu.roll(colflow[i], cols - 1 - d, 1), x)
                for i, x in ((2, total), (3, water))]
        flow = flow + (high[1] - low[1])
        out = out + (jnp.maximum(high[0], 0.0) + jnp.maximum(-low[0], 0.0))
        net[d] = flow
        return above_total, above_water, jnp.maximum(most, out)

    _, _, most = lax.fori_loop(0, depth, transport, (under_total, under_water, nothing))

    maxw[w] = jnp.max(most.reshape(rows // brick_rows, brick_rows, cols), axis=0)
    everyone("wide", lambda peer: maxw.at[w], lambda sender: maxw.at[sender])()
    maxn[k] = jnp.max(maxw[...], axis=0)
    everyone("narrow", lambda peer: maxn.at[k], lambda sender: maxn.at[sender])()
    top_rate = jnp.max(jnp.max(maxn[...], axis=0), axis=(0, 1), keepdims=True)
    step_size = courant / (top_rate + tiny)

    def update(d, carry):
        s = sat_ref[d] - step_size * net[d] + step_size * source[...]
        satnew_ref[d] = s
        value = fields[d + 1, 1] * (gains[d, 0] * s * s + gains[d, 1] * (1.0 - s) * (1.0 - s))
        at = pl.multiple_of(d * brick_rows, brick_rows)
        for p in range(n_wide):
            slab[p, pl.ds(at, brick_rows), :] = value[p * brick_rows:(p + 1) * brick_rows]
        return carry

    lax.fori_loop(0, depth, update, 0)

    def part(sender):
        return coef.at[pl.ds(pl.multiple_of(sender * band, band), band), :]

    wait_bricks = everyone("wide", lambda peer: slab.at[peer], part)
    coef[pl.ds(pl.multiple_of(w * band, band), band), :] = slab[w]
    wait_bricks()

    last_row = brick_rows - 1

    def send_sides(ref, which):
        rowsend[0, which] = ref[pl.ds(0, layers, stride=brick_rows), :]
        rowsend[1, which] = ref[pl.ds(last_row, layers, stride=brick_rows), :]
        wait_rows = neighbours(
            "wide", rowsend.at[0, which], rowsend.at[1, which],
            rowhalo.at[0, which], rowhalo.at[1, which],
        )
        for t in range(tiles):
            def collect(i, carry):
                low, high = carry
                for u in range(4):
                    z = i * 4 + u
                    at = pl.multiple_of((t * cols + z) * brick_rows, brick_rows)
                    turned = pltpu.roll(ref[pl.ds(at, brick_rows), :], z, 1)
                    low = jnp.where(tlane == z, turned, low)
                    high = jnp.where(tlane == lax.rem(z + cols - 1, cols), turned, high)
                return low, high

            low, high = lax.fori_loop(0, cols // 4, collect, (zero, zero))
            packs[0, which, pl.ds(t * brick_rows, brick_rows), :] = low
            packs[1, which, pl.ds(t * brick_rows, brick_rows), :] = pltpu.roll(high, 1, 1)
        wait_packs = neighbours(
            "narrow", packs.at[0, which], packs.at[1, which],
            packhalo.at[0, which], packhalo.at[1, which],
        )
        return wait_rows, wait_packs

    wait_rows, wait_packs = send_sides(coef, 0)

    unroll = 4

    def at_layer(z):
        return pl.ds(pl.multiple_of(z * brick_rows, brick_rows), brick_rows)

    def assemble(i, carry):
        below, here, total = carry
        for u in range(unroll):
            z = i * unroll + u
            above = coef[at_layer(z + 1), :]
            df = jnp.where(z < layers - 1, harmonic(here, above), zero)
            rf = jnp.where(trow == last_row, 0.0, harmonic(here, pltpu.roll(here, last_row, 0)))
            cf = jnp.where(tlane == cols - 1, 0.0, harmonic(here, pltpu.roll(here, cols - 1, 1)))
            diag = (
                compress * here + below + df + pltpu.roll(rf, 1, 0) + rf + pltpu.roll(cf, 1, 1) + cf
            )
            sc = relax / diag
            dface[at_layer(z), :] = df
            rface[at_layer(z), :] = rf
            cface[at_layer(z), :] = cf
            scale[at_layer(z), :] = sc
            v = sc * res_ref[z]
            first[at_layer(z), :] = v
            va[at_layer(z), :] = v
            total = total + here
            below, here = df, above
        return below, here, total

    _, _, coef_total = lax.fori_loop(
        0, layers // unroll, assemble, (zero, coef[pl.ds(0, brick_rows), :], zero)
    )

    def sweep(src, dst):
        def body(i, carry):
            v_below, d_below, v = carry
            for u in range(unroll):
                z = i * unroll + u
                v_above = src[at_layer(z + 1), :]
                df = dface[at_layer(z), :]
                rf = rface[at_layer(z), :]
                cf = cface[at_layer(z), :]
                off = (
                    d_below * v_below + df * v_above
                    + pltpu.roll(rf * v, 1, 0) + rf * pltpu.roll(v, last_row, 0)
                    + pltpu.roll(cf * v, 1, 1) + cf * pltpu.roll(v, cols - 1, 1)
                )
                dst[at_layer(z), :] = (
                    (1.0 - relax) * v + first[at_layer(z), :] + scale[at_layer(z), :] * off
                )
                v_below, d_below, v = v, df, v_above
            return v_below, d_below, v

        lax.fori_loop(0, layers // unroll, body, (zero, zero, src[pl.ds(0, brick_rows), :]))

    def coarse_row():
        wait_rows()
        wait_packs()

        def side(own, halo, present):
            return jnp.where(present, jnp.sum(harmonic(own, halo), axis=(0, 1), keepdims=True), 0.0)

        low_rows = side(rowsend[0, 0], rowhalo[0, 0], has_below)
        high_rows = side(rowsend[1, 0], rowhalo[1, 0], has_above)
        low_cols = side(packs[0, 0], packhalo[0, 0], has_left)
        high_cols = side(packs[1, 0], packhalo[1, 0], has_right)
        diagonal = (
            compress * jnp.sum(coef_total, axis=(0, 1), keepdims=True)
            + low_rows + high_rows + low_cols + high_cols
        )
        total = jnp.sum(res_total, axis=(0, 1), keepdims=True)
        message = zero
        for i, value in enumerate((total, diagonal, low_rows, high_rows, low_cols, high_cols)):
            message = jnp.where(tlane == i, value, message)
        cw[pl.ds(pl.multiple_of(w * brick_rows, brick_rows), brick_rows), :] = message

        def at_wide(sender):
            return cw.at[pl.ds(pl.multiple_of(sender * brick_rows, brick_rows), brick_rows), :]

        return everyone("wide", lambda peer: at_wide(w), at_wide)

    def coarse_gather():
        cn[pl.ds(pl.multiple_of(k * n_wide, n_wide), n_wide), :] = cw[
            pl.ds(0, n_wide, stride=brick_rows), :
        ]

        def at_narrow(sender):
            return cn.at[pl.ds(pl.multiple_of(sender * n_wide, n_wide), n_wide), :]

        return everyone("narrow", lambda peer: at_narrow(k), at_narrow)

    bricks = n_wide * n_narrow
    blane = lax.broadcasted_iota(jnp.int32, (bricks, cols), 1)
    brow = lax.broadcasted_iota(jnp.int32, (bricks, cols), 0)

    def coarse_build():
        gathered = cn[...]
        matrix = jnp.where(blane == brow, gathered[:, 1:2], 0.0)
        for i, away in ((2, -1), (3, 1), (4, -n_wide), (5, n_wide)):
            matrix = jnp.where(blane == brow + away, matrix - gathered[:, i:i + 1], matrix)
        mat[...] = matrix
        rhs[...] = jnp.broadcast_to(gathered[:, 0:1], (bricks, cols))

    mine = k * n_wide + w

    def eliminate(j, carry):
        matrix = mat[...]
        right = rhs[...]
        pivot_row = mat[pl.ds(j, 1), :]
        pivot_rhs = rhs[pl.ds(j, 1), :]
        column = jnp.sum(jnp.where(blane == j, matrix, 0.0), axis=1, keepdims=True)
        pivot = jnp.sum(jnp.where(blane[:1] == j, pivot_row, 0.0), axis=1, keepdims=True)
        factor = jnp.where((brow == j) | (j == mine), 0.0, column / pivot)
        mat[...] = matrix - factor * pivot_row
        rhs[...] = right - factor * pivot_rhs
        return carry

    wait_gather = coarse_row_wait = None
    src, dst = va, vb
    for number in range(SWEEPS - 1):
        if number == 1:
            coarse_row_wait = coarse_row()
        if number == 3:
            coarse_row_wait()
            wait_gather = coarse_gather()
        sweep(src, dst)
        src, dst = dst, src
    wait_value_rows, wait_value_packs = send_sides(src, 1)

    wait_gather()
    coarse_build()
    lax.fori_loop(0, bricks, eliminate, 0)
    own_row = mat[pl.ds(mine, 1), :]
    own_pivot = jnp.sum(jnp.where(blane[:1] == mine, own_row, 0.0), axis=1, keepdims=True)
    coarse_value = rhs[pl.ds(mine, 1), :] / own_pivot

    wait_value_rows()
    wait_value_packs()
    for side, present in ((0, has_below), (1, has_above)):
        c = jnp.where(present, rowhalo[side, 0], 0.0)
        rowterm[side, 0] = c
        rowterm[side, 1] = jnp.where(present, c * rowhalo[side, 1], 0.0)
    for side, present in ((0, has_left), (1, has_right)):
        c = jnp.where(present, packhalo[side, 0], 0.0)
        packterm[side, 0] = c
        packterm[side, 1] = jnp.where(present, c * packhalo[side, 1], 0.0)

    for t in range(tiles):
        tile = pl.ds(t * brick_rows, brick_rows)

        def average(i, carry):
            for u in range(unroll):
                z = i * unroll + u
                layer = t * cols + z
                c = coef[at_layer(layer), :]
                sums = [c, c * src[at_layer(layer), :]]
                for j in range(2):
                    low = rowterm[0, j, pl.ds(layer, 1), :]
                    high = rowterm[1, j, pl.ds(layer, 1), :]
                    left = pltpu.roll(packterm[0, j, tile, :], lax.rem(cols - z, cols), 1)
                    right = pltpu.roll(packterm[1, j, tile, :], cols - 1 - z, 1)
                    sums[j] = (
                        sums[j]
                        + jnp.where(trow == 0, low, 0.0) + jnp.where(trow == last_row, high, 0.0)
                        + jnp.where(tlane == 0, left, 0.0)
                        + jnp.where(tlane == cols - 1, right, 0.0)
                    )
                prec_ref[layer] = sums[1] / sums[0] + coarse_value
            return carry

        lax.fori_loop(0, cols // unroll, average, 0)


def shards(n_wide, n_narrow, *args):
    sat, residual = args[0], args[6]
    depth, rows, cols = sat.shape
    layers, brick_rows, _ = residual.shape
    tiles = layers // cols
    bricks = n_wide * n_narrow
    cells = layers * brick_rows
    copies = 3 * 4 + 3 * (n_wide - 1) + 2 * (n_narrow - 1)
    vmem = pl.BlockSpec(memory_space=pltpu.VMEM)
    smem = pl.BlockSpec(memory_space=pltpu.SMEM)

    def buffer(*shape):
        return pltpu.VMEM(shape, F32)

    return pl.pallas_call(
        functools.partial(kernel, n_wide, n_narrow),
        out_shape=(
            jax.ShapeDtypeStruct(sat.shape, F32),
            jax.ShapeDtypeStruct(residual.shape, F32),
        ),
        in_specs=[vmem, vmem, vmem, smem, smem, smem, vmem],
        out_specs=(vmem, vmem),
        scratch_shapes=[
            buffer(depth + 2, 3, rows, cols),
            buffer(depth, 2, rows, cols),
            buffer(depth, rows, cols),
            buffer(2, rows, cols),
            buffer(2, rows, cols),
            buffer(4, rows, cols),
            buffer(rows, cols),
            buffer(n_wide, brick_rows, cols),
            buffer(n_narrow, brick_rows, cols),
            buffer(n_wide, depth * brick_rows, cols),
            buffer(cells + brick_rows, cols),
            buffer(cells, cols),
            buffer(cells, cols),
            buffer(cells, cols),
            buffer(cells, cols),
            buffer(cells, cols),
            buffer(cells + brick_rows, cols),
            buffer(cells + brick_rows, cols),
            buffer(2, 2, layers, cols),
            buffer(2, 2, layers, cols),
            buffer(2, 2, layers, cols),
            buffer(2, 2, tiles * brick_rows, cols),
            buffer(2, 2, tiles * brick_rows, cols),
            buffer(2, 2, tiles * brick_rows, cols),
            buffer(n_wide * brick_rows, cols),
            buffer(bricks, cols),
            buffer(bricks, cols),
            buffer(bricks, cols),
            pltpu.SemaphoreType.DMA((copies,)),
            pltpu.SemaphoreType.DMA((copies,)),
        ],
        compiler_params=pltpu.CompilerParams(
            collective_id=0, has_side_effects=True, vmem_limit_bytes=40 * 1024 * 1024
        ),
    )(*args)


def solution(mesh):
    placed = (
        P("wide", None, "narrow"),
        P("wide", None, "narrow"),
        P("wide", None, "narrow"),
        P(),
        P(),
        P(),
        P(None, "wide", "narrow"),
    )
    return jax.shard_map(
        functools.partial(shards, mesh.shape["wide"], mesh.shape["narrow"]),
        mesh=mesh,
        in_specs=placed,
        out_specs=(P("wide", None, "narrow"), P(None, "wide", "narrow")),
        check_vma=False,
    )
```

time: 240 us -> 64.9 us (0.27); the launches traced: 236 us -> 64.6 us
  blocking collectives: 81.3 us -> 0 us
  other arithmetic: 70.7 us -> 0 us
  Pallas kernels: 0 us -> 56.2 us
  starting transfers between devices: 34.6 us -> 0 us
  local copies, waits for them, and re-layouts: 33.9 us -> 7.74 us
  waiting for transfers between devices: 10.2 us -> 0 us
  between operations: 4.98 us -> 0.66 us
    pallas_call x0 -> x1, Pallas kernels: none -> 56.2 us  [shards(): pl.pallas_call(functools.partial(kernel, n_wide, n_narrow), out_shape=(ja...]
    unnamed x1 -> x0, blocking collectives: 42 us -> none
    pmax x1 -> x0, blocking collectives: 39.3 us -> none  [shards(): top_rate = lax.pmax(jnp.max(outflow), ('wide', 'narrow'))]
    another operation x7 -> x0, other arithmetic: 29.2 us -> none  [the longest x2 22.4 us: shards(): stacked = jnp.stack([pressure, perm_cell, water_frac])]
    ppermute x10 -> x0, starting transfers between devices: 29.1 us -> none  [the longest x5 19.9 us: extended_2(): lax.ppermute(lax.slice_in_dim(block, block.shape[dim] - width, None, axis...]
    slice x19 -> x0, local copies, waits for them, and re-layouts: 16.1 us -> none  [the longest x3 5.93 us: rock_lookup(): oil_gain = jnp.where(matched, rock_table[2, number], oil_gain)]
    select_n x2 -> x0, other arithmetic: 12.7 us -> none  [the longest x1 12.7 us: rock_lookup(): perm_cell = jnp.where(matched, rock_table[0, number], perm_cell)]
    mul x6 -> x0, other arithmetic: 10.1 us -> none  [the longest x3 5.49 us: flows_between(): total_flow * jnp.where(total_flow > 0, lower_side[2], upper_side[2])]
  transfers between devices with their start and end apart: 11 -> 0, of which waited for: 4 -> 0; matrix products, arithmetic and copies ran while one was open for 5% -> 0% of each run, Pallas kernels for 0% -> 0%
where the time goes in v1:
time: 64.9 us; the launch traced here: 64.6 us
  Pallas kernels  56.2 us (87%)
  local copies, waits for them, and re-layouts  7.74 us (12%)
  between operations  0.66 us (1%)
    pallas_call x1, Pallas kernels, shards(): pl.pallas_call(functools.partial(kernel, n_wide, n_narrow), out_shape=(ja...  56.2 us
    unnamed x16, local copies, waits for them, and re-layouts  7.74 us

profile of v1, /device:TPU:1, one launch (start us, length us, event | category | flops | bytes accessed | tf_op | source)
XLA Modules:
  0.0 64.6 jit_solution(7629039482418568300)
XLA Ops:
  0.6 0.0 copy-start
  0.6 1.0 %copy-done = f32[16,64,128]{2,1,0:T(8,128)S(1)} copy-done((f32[16,64,128]{2,1,0:T(8,128)S(1)}, f32[16,64,128]{2,1,0:T(8,128)}, u32[]{:S(2)}) %copy-start) | copy-done | bytes 524312
  1.7 0.0 copy-start.1
  1.7 1.0 %copy-done.1 = f32[16,64,128]{2,1,0:T(8,128)S(1)} copy-done((f32[16,64,128]{2,1,0:T(8,128)S(1)}, f32[16,64,128]{2,1,0:T(8,128)}, u32[]{:S(2)}) %copy-start.1) | copy-done | bytes 524312
  2.7 0.0 copy-start.2
  2.7 1.0 %copy-done.2 = s32[16,64,128]{2,1,0:T(8,128)S(1)} copy-done((s32[16,64,128]{2,1,0:T(8,128)S(1)}, s32[16,64,128]{2,1,0:T(8,128)}, u32[]{:S(2)}) %copy-start.2) | copy-done | bytes 524312
  3.8 0.0 copy-start.3
  3.8 1.0 %copy-done.3 = f32[128,8,128]{2,1,0:T(8,128)S(1)} copy-done((f32[128,8,128]{2,1,0:T(8,128)S(1)}, f32[128,8,128]{2,1,0:T(8,128)}, u32[]{:S(2)}) %copy-start.3) | copy-done | bytes 524312
  4.8 0.0 copy-start.4
  4.8 0.7 %copy-done.4 = f32[3,16]{1,0:T(4,128)S(1)} copy-done((f32[3,16]{1,0:T(4,128)S(1)}, f32[3,16]{1,0:T(4,128)}, u32[]{:S(2)}) %copy-start.4) | copy-done | bytes 216
  5.5 0.0 copy-start.5
  5.5 0.7 %copy-done.5 = s32[64]{0:T(128)S(1)} copy-done((s32[64]{0:T(128)S(1)}, s32[64]{0:T(128)}, u32[]{:S(2)}) %copy-start.5) | copy-done | bytes 280
  6.1 0.0 copy-start.6
  6.1 0.7 %copy-done.6 = f32[64]{0:T(128)S(1)} copy-done((f32[64]{0:T(128)S(1)}, f32[64]{0:T(128)}, u32[]{:S(2)}) %copy-start.6) | copy-done | bytes 280
  6.8 56.2 %shard_map.86 = (f32[16,64,128]{2,1,0:T(8,128)S(1)}, f32[128,8,128]{2,1,0:T(8,128)S(1)}) custom-call(f32[16,64,128]{2,1,0:T(8,128)S(1)} %copy-done, f32[16,64,128]{2,1,0:T(8,128)S(1)} %copy-done.1, s32[16,64,128]{2,1,0:T(8,128)S(1)} %copy-done.2, f32[3,16]{1,0:T(4,128)S(1)} %copy-done.4, s32[64]{0:T(128)S(1)} %copy-done.5, f32[64]{0:T(128)S(1)} %copy-done.6, ...), custom_call_target="tpu_custom_call" | custom-call | tf_op jit(solution)/shard_map/pallas_call | solution.py:501
  63.0 0.8 %copy.11 = f32[16,64,128]{2,1,0:T(8,128)} copy(f32[16,64,128]{2,1,0:T(8,128)S(1)} %get-tuple-element.4) | data formatting | bytes 1048576
  63.8 0.8 %copy.12 = f32[128,8,128]{2,1,0:T(8,128)} copy(f32[128,8,128]{2,1,0:T(8,128)S(1)} %get-tuple-element.5) | data formatting | bytes 1048576
Async XLA Ops:
  0.6 1.0 %copy-start = (f32[16,64,128]{2,1,0:T(8,128)S(1)}, f32[16,64,128]{2,1,0:T(8,128)}, u32[]{:S(2)}) copy-start(f32[16,64,128]{2,1,0:T(8,128)} %sat_ref.1) | copy-start | bytes 1572868
  1.7 1.0 %copy-start.1 = (f32[16,64,128]{2,1,0:T(8,128)S(1)}, f32[16,64,128]{2,1,0:T(8,128)}, u32[]{:S(2)}) copy-start(f32[16,64,128]{2,1,0:T(8,128)} %pres_ref.1) | copy-start | bytes 1572868
  2.7 1.0 %copy-start.2 = (s32[16,64,128]{2,1,0:T(8,128)S(1)}, s32[16,64,128]{2,1,0:T(8,128)}, u32[]{:S(2)}) copy-start(s32[16,64,128]{2,1,0:T(8,128)} %rock_ref.1) | copy-start | bytes 1572868
  3.8 1.0 %copy-start.3 = (f32[128,8,128]{2,1,0:T(8,128)S(1)}, f32[128,8,128]{2,1,0:T(8,128)}, u32[]{:S(2)}) copy-start(f32[128,8,128]{2,1,0:T(8,128)} %res_ref.1) | copy-start | bytes 1572868
  4.8 0.7 %copy-start.4 = (f32[3,16]{1,0:T(4,128)S(1)}, f32[3,16]{1,0:T(4,128)}, u32[]{:S(2)}) copy-start(f32[3,16]{1,0:T(4,128)} %table_ref.1) | copy-start | bytes 580
  5.5 0.7 %copy-start.5 = (s32[64]{0:T(128)S(1)}, s32[64]{0:T(128)}, u32[]{:S(2)}) copy-start(s32[64]{0:T(128)} %wcol_ref.1) | copy-start | bytes 772
  6.1 0.7 %copy-start.6 = (f32[64]{0:T(128)S(1)}, f32[64]{0:T(128)}, u32[]{:S(2)}) copy-start(f32[64]{0:T(128)} %wrate_ref.1) | copy-start | bytes 772

commit v2 on v1

--- a/solution.py
+++ b/solution.py
@@ -36,12 +36,13 @@
 
 def kernel(
     n_wide, n_narrow,
+    sat_in, pres_in, rock_in, table_in, wcol_in, wrate_in, res_in,
+    satnew_ref, prec_ref,
     sat_ref, pres_ref, rock_ref, table_ref, wcol_ref, wrate_ref, res_ref,
-    satnew_ref, prec_ref,
     fields, gains, net, colpack, colhalo, colflow, source, maxw, maxn,
     slab, coef, dface, rface, cface, scale, first, va, vb,
-    rowsend, rowhalo, rowterm, packs, packhalo, packterm, cw, cn, mat, rhs,
-    sends, recvs,
+    rowsend, rowhalo, rowterm, packs, packhalo, packterm, cw, cn, sidepack, sidehalo,
+    loads, sends, recvs,
 ):
     depth, rows, cols = sat_ref.shape
     layers, brick_rows, _ = res_ref.shape
@@ -54,6 +55,16 @@
     size = {"wide": n_wide, "narrow": n_narrow}
     count = [0]
 
+    loading = [
+        pltpu.make_async_copy(src, dst, loads.at[i])
+        for i, (src, dst) in enumerate((
+            (table_in, table_ref), (rock_in, rock_ref), (sat_in, sat_ref), (pres_in, pres_ref),
+            (wcol_in, wcol_ref), (wrate_in, wrate_ref), (res_in, res_ref),
+        ))
+    ]
+    for copy in loading:
+        copy.start()
+
     def slot():
         count[0] += 1
         return count[0] - 1
@@ -136,11 +147,13 @@
 
     @pl.when(k == 0)
     def _():
+        sidehalo[0] = jnp.ones((rows, cols), F32)
         colhalo[0] = jnp.ones((rows, cols), F32)
         packhalo[0] = jnp.ones((2, tiles * brick_rows, cols), F32)
 
     @pl.when(k == n_narrow - 1)
     def _():
+        sidehalo[1] = jnp.ones((rows, cols), F32)
         colhalo[1] = jnp.ones((rows, cols), F32)
         packhalo[1] = jnp.ones((2, tiles * brick_rows, cols), F32)
 
@@ -149,6 +162,8 @@
     vb[pl.ds(layers * brick_rows, brick_rows), :] = zero
 
     rocks = table_ref.shape[1]
+    for copy in loading[:4]:
+        copy.wait()
 
     def derive(d, carry):
         packed_low, packed_high = carry
@@ -189,19 +204,25 @@
 
     all_cols = cols * n_narrow
 
+    for copy in loading[4:]:
+        copy.wait()
+    cell = row * cols + lane
+
     def well(i, total):
-        column = wcol_ref[i]
-        inside = column % all_cols - k * cols
-        return total + jnp.where(
-            (row == column // all_cols) & (lane == inside), wrate_ref[i], 0.0
-        )
-
-    source[...] = lax.fori_loop(0, wcol_ref.shape[0], well, jnp.zeros((rows, cols), F32))
-
-    def add_res(z, total):
-        return total + res_ref[z]
-
-    res_total = lax.fori_loop(0, layers, add_res, zero)
+        for u in range(8):
+            column = wcol_ref[i * 8 + u]
+            inside = lax.rem(column, all_cols) - k * cols
+            target = lax.div(column, all_cols) * cols + inside
+            target = jnp.where((inside >= 0) & (inside < cols), target, -1)
+            total = total + jnp.where(cell == target, wrate_ref[i * 8 + u], 0.0)
+        return total
+
+    source[...] = lax.fori_loop(0, wcol_ref.shape[0] // 8, well, jnp.zeros((rows, cols), F32))
+
+    def add_res(i, total):
+        return total + jnp.sum(res_ref[pl.ds(i * 16, 16)], axis=0)
+
+    res_total = jnp.sum(lax.fori_loop(0, layers // 16, add_res, zero), axis=(0, 1), keepdims=True)
 
     wait_cols()
 
@@ -264,21 +285,62 @@
     step_size = courant / (top_rate + tiny)
 
     def update(d, carry):
+        total, cross, packed_low, packed_high = carry
         s = sat_ref[d] - step_size * net[d] + step_size * source[...]
         satnew_ref[d] = s
         value = fields[d + 1, 1] * (gains[d, 0] * s * s + gains[d, 1] * (1.0 - s) * (1.0 - s))
         at = pl.multiple_of(d * brick_rows, brick_rows)
         for p in range(n_wide):
             slab[p, pl.ds(at, brick_rows), :] = value[p * brick_rows:(p + 1) * brick_rows]
-        return carry
-
-    lax.fori_loop(0, depth, update, 0)
+        turned = pltpu.roll(value, d, 1)
+        packed_low = jnp.where(lane == d, turned, packed_low)
+        packed_high = jnp.where(lane == lax.rem(d + cols - 1, cols), turned, packed_high)
+        cross = cross + harmonic(value, pltpu.roll(value, rows - 1, 0))
+        return total + value, cross, packed_low, packed_high
+
+    total, cross, packed_low, packed_high = lax.fori_loop(
+        0, depth, update, (nothing, nothing, blank, blank)
+    )
+    sidepack[0] = packed_low
+    sidepack[1] = pltpu.roll(packed_high, 1, 1)
+    wait_sides = neighbours(
+        "narrow", sidepack.at[0], sidepack.at[1], sidehalo.at[0], sidehalo.at[1]
+    )
 
     def part(sender):
         return coef.at[pl.ds(pl.multiple_of(sender * band, band), band), :]
 
     wait_bricks = everyone("wide", lambda peer: slab.at[peer], part)
     coef[pl.ds(pl.multiple_of(w * band, band), band), :] = slab[w]
+
+    brick_count = n_wide
+
+    def by_brick(block):
+        summed = jnp.sum(block.reshape(brick_count, brick_rows, cols), axis=1)
+        return jnp.sum(summed, axis=1, keepdims=True)
+
+    clane = lax.broadcasted_iota(jnp.int32, (brick_count, cols), 1)
+    crow = lax.broadcasted_iota(jnp.int32, (brick_count, cols), 0)
+    high_rows = by_brick(jnp.where((lax.rem(row, brick_rows) == brick_rows - 1) & (row < rows - 1), cross, 0.0))
+    low_rows = by_brick(
+        pltpu.roll(jnp.where((lax.rem(row, brick_rows) == brick_rows - 1) & (row < rows - 1), cross, 0.0), 1, 0)
+    )
+    coef_sum = by_brick(total)
+    wait_sides()
+    low_cols = by_brick(jnp.where((lane < depth) & has_left, harmonic(sidepack[0], sidehalo[0]), 0.0))
+    high_cols = by_brick(jnp.where((lane < depth) & has_right, harmonic(sidepack[1], sidehalo[1]), 0.0))
+    diagonal = compress * coef_sum + low_rows + high_rows + low_cols + high_cols
+    message = jnp.where((clane == 0) & (crow == w), res_total, 0.0)
+    for i, value in enumerate((diagonal, low_rows, high_rows, low_cols, high_cols)):
+        message = jnp.where(clane == i + 1, value, message)
+    cw[w] = message
+    everyone("wide", lambda peer: cw.at[w], lambda sender: cw.at[sender])()
+
+    def at_narrow(sender):
+        return cn.at[pl.ds(pl.multiple_of(sender * n_wide, n_wide), n_wide), :]
+
+    cn[pl.ds(pl.multiple_of(k * n_wide, n_wide), n_wide), :] = jnp.sum(cw[...], axis=0)
+    wait_coarse = everyone("narrow", lambda peer: at_narrow(k), at_narrow)
     wait_bricks()
 
     last_row = brick_rows - 1
@@ -293,15 +355,15 @@
         for t in range(tiles):
             def collect(i, carry):
                 low, high = carry
-                for u in range(4):
-                    z = i * 4 + u
+                for u in range(32):
+                    z = i * 32 + u
                     at = pl.multiple_of((t * cols + z) * brick_rows, brick_rows)
                     turned = pltpu.roll(ref[pl.ds(at, brick_rows), :], z, 1)
                     low = jnp.where(tlane == z, turned, low)
                     high = jnp.where(tlane == lax.rem(z + cols - 1, cols), turned, high)
                 return low, high
 
-            low, high = lax.fori_loop(0, cols // 4, collect, (zero, zero))
+            low, high = lax.fori_loop(0, cols // 32, collect, (zero, zero))
             packs[0, which, pl.ds(t * brick_rows, brick_rows), :] = low
             packs[1, which, pl.ds(t * brick_rows, brick_rows), :] = pltpu.roll(high, 1, 1)
         wait_packs = neighbours(
@@ -312,13 +374,13 @@
 
     wait_rows, wait_packs = send_sides(coef, 0)
 
-    unroll = 4
+    unroll = 16
 
     def at_layer(z):
         return pl.ds(pl.multiple_of(z * brick_rows, brick_rows), brick_rows)
 
     def assemble(i, carry):
-        below, here, total = carry
+        below, here = carry
         for u in range(unroll):
             z = i * unroll + u
             above = coef[at_layer(z + 1), :]
@@ -336,19 +398,16 @@
             v = sc * res_ref[z]
             first[at_layer(z), :] = v
             va[at_layer(z), :] = v
-            total = total + here
             below, here = df, above
-        return below, here, total
-
-    _, _, coef_total = lax.fori_loop(
-        0, layers // unroll, assemble, (zero, coef[pl.ds(0, brick_rows), :], zero)
-    )
+        return below, here
+
+    lax.fori_loop(0, layers // unroll, assemble, (zero, coef[pl.ds(0, brick_rows), :]))
 
     def sweep(src, dst):
         def body(i, carry):
             v_below, d_below, v = carry
-            for u in range(unroll):
-                z = i * unroll + u
+            for u in range(32):
+                z = i * 32 + u
                 v_above = src[at_layer(z + 1), :]
                 df = dface[at_layer(z), :]
                 rf = rface[at_layer(z), :]
@@ -364,89 +423,41 @@
                 v_below, d_below, v = v, df, v_above
             return v_below, d_below, v
 
-        lax.fori_loop(0, layers // unroll, body, (zero, zero, src[pl.ds(0, brick_rows), :]))
-
-    def coarse_row():
-        wait_rows()
-        wait_packs()
-
-        def side(own, halo, present):
-            return jnp.where(present, jnp.sum(harmonic(own, halo), axis=(0, 1), keepdims=True), 0.0)
-
-        low_rows = side(rowsend[0, 0], rowhalo[0, 0], has_below)
-        high_rows = side(rowsend[1, 0], rowhalo[1, 0], has_above)
-        low_cols = side(packs[0, 0], packhalo[0, 0], has_left)
-        high_cols = side(packs[1, 0], packhalo[1, 0], has_right)
-        diagonal = (
-            compress * jnp.sum(coef_total, axis=(0, 1), keepdims=True)
-            + low_rows + high_rows + low_cols + high_cols
-        )
-        total = jnp.sum(res_total, axis=(0, 1), keepdims=True)
-        message = zero
-        for i, value in enumerate((total, diagonal, low_rows, high_rows, low_cols, high_cols)):
-            message = jnp.where(tlane == i, value, message)
-        cw[pl.ds(pl.multiple_of(w * brick_rows, brick_rows), brick_rows), :] = message
-
-        def at_wide(sender):
-            return cw.at[pl.ds(pl.multiple_of(sender * brick_rows, brick_rows), brick_rows), :]
-
-        return everyone("wide", lambda peer: at_wide(w), at_wide)
-
-    def coarse_gather():
-        cn[pl.ds(pl.multiple_of(k * n_wide, n_wide), n_wide), :] = cw[
-            pl.ds(0, n_wide, stride=brick_rows), :
-        ]
-
-        def at_narrow(sender):
-            return cn.at[pl.ds(pl.multiple_of(sender * n_wide, n_wide), n_wide), :]
-
-        return everyone("narrow", lambda peer: at_narrow(k), at_narrow)
+        lax.fori_loop(0, layers // 32, body, (zero, zero, src[pl.ds(0, brick_rows), :]))
 
     bricks = n_wide * n_narrow
     blane = lax.broadcasted_iota(jnp.int32, (bricks, cols), 1)
     brow = lax.broadcasted_iota(jnp.int32, (bricks, cols), 0)
 
-    def coarse_build():
+    mine = k * n_wide + w
+
+    def coarse_solve():
         gathered = cn[...]
         matrix = jnp.where(blane == brow, gathered[:, 1:2], 0.0)
         for i, away in ((2, -1), (3, 1), (4, -n_wide), (5, n_wide)):
             matrix = jnp.where(blane == brow + away, matrix - gathered[:, i:i + 1], matrix)
-        mat[...] = matrix
-        rhs[...] = jnp.broadcast_to(gathered[:, 0:1], (bricks, cols))
-
-    mine = k * n_wide + w
-
-    def eliminate(j, carry):
-        matrix = mat[...]
-        right = rhs[...]
-        pivot_row = mat[pl.ds(j, 1), :]
-        pivot_rhs = rhs[pl.ds(j, 1), :]
-        column = jnp.sum(jnp.where(blane == j, matrix, 0.0), axis=1, keepdims=True)
-        pivot = jnp.sum(jnp.where(blane[:1] == j, pivot_row, 0.0), axis=1, keepdims=True)
-        factor = jnp.where((brow == j) | (j == mine), 0.0, column / pivot)
-        mat[...] = matrix - factor * pivot_row
-        rhs[...] = right - factor * pivot_rhs
-        return carry
-
-    wait_gather = coarse_row_wait = None
+        right = jnp.broadcast_to(gathered[:, 0:1], (bricks, cols))
+        for j in range(bricks):
+            column = jnp.broadcast_to(matrix[:, j:j + 1], (bricks, cols))
+            factor = jnp.where(brow == j, 0.0, column / column[j:j + 1])
+            matrix, right = (
+                matrix - factor * matrix[j:j + 1], right - factor * right[j:j + 1]
+            )
+        own = brow == mine
+        pivot = jnp.sum(jnp.where(own & (blane == mine), matrix, 0.0), axis=(0, 1), keepdims=True)
+        answer = jnp.sum(jnp.where(own & (blane == 0), right, 0.0), axis=(0, 1), keepdims=True)
+        return answer / pivot
+
     src, dst = va, vb
     for number in range(SWEEPS - 1):
-        if number == 1:
-            coarse_row_wait = coarse_row()
-        if number == 3:
-            coarse_row_wait()
-            wait_gather = coarse_gather()
         sweep(src, dst)
         src, dst = dst, src
     wait_value_rows, wait_value_packs = send_sides(src, 1)
-
-    wait_gather()
-    coarse_build()
-    lax.fori_loop(0, bricks, eliminate, 0)
-    own_row = mat[pl.ds(mine, 1), :]
-    own_pivot = jnp.sum(jnp.where(blane[:1] == mine, own_row, 0.0), axis=1, keepdims=True)
-    coarse_value = rhs[pl.ds(mine, 1), :] / own_pivot
-
+    wait_coarse()
+    coarse_value = coarse_solve()
+
+    wait_rows()
+    wait_packs()
     wait_value_rows()
     wait_value_packs()
     for side, present in ((0, has_below), (1, has_above)):
@@ -491,9 +502,10 @@
     tiles = layers // cols
     bricks = n_wide * n_narrow
     cells = layers * brick_rows
-    copies = 3 * 4 + 3 * (n_wide - 1) + 2 * (n_narrow - 1)
+    copies = 2 * 7 + 3 * (n_wide - 1) + 2 * (n_narrow - 1)
     vmem = pl.BlockSpec(memory_space=pltpu.VMEM)
-    smem = pl.BlockSpec(memory_space=pltpu.SMEM)
+    anywhere = pl.BlockSpec(memory_space=pl.ANY)
+    table, wells = args[3].shape, args[4].shape
 
     def buffer(*shape):
         return pltpu.VMEM(shape, F32)
@@ -504,9 +516,16 @@
             jax.ShapeDtypeStruct(sat.shape, F32),
             jax.ShapeDtypeStruct(residual.shape, F32),
         ),
-        in_specs=[vmem, vmem, vmem, smem, smem, smem, vmem],
+        in_specs=[anywhere] * 7,
         out_specs=(vmem, vmem),
         scratch_shapes=[
+            buffer(*sat.shape),
+            buffer(*sat.shape),
+            pltpu.VMEM(sat.shape, jnp.int32),
+            pltpu.SMEM(table, F32),
+            pltpu.SMEM(wells, jnp.int32),
+            pltpu.SMEM(wells, F32),
+            buffer(*residual.shape),
             buffer(depth + 2, 3, rows, cols),
             buffer(depth, 2, rows, cols),
             buffer(depth, rows, cols),
@@ -531,15 +550,16 @@
             buffer(2, 2, tiles * brick_rows, cols),
             buffer(2, 2, tiles * brick_rows, cols),
             buffer(2, 2, tiles * brick_rows, cols),
-            buffer(n_wide * brick_rows, cols),
+            buffer(n_wide, n_wide, cols),
             buffer(bricks, cols),
-            buffer(bricks, cols),
-            buffer(bricks, cols),
+            buffer(2, rows, cols),
+            buffer(2, rows, cols),
+            pltpu.SemaphoreType.DMA((7,)),
             pltpu.SemaphoreType.DMA((copies,)),
             pltpu.SemaphoreType.DMA((copies,)),
         ],
         compiler_params=pltpu.CompilerParams(
-            collective_id=0, has_side_effects=True, vmem_limit_bytes=40 * 1024 * 1024
+            collective_id=0, has_side_effects=True, vmem_limit_bytes=56 * 1024 * 1024
         ),
     )(*args)
 

time: 64.9 us -> 45.4 us (0.70)
  Pallas kernels: 56.2 us -> 41.5 us
  local copies, waits for them, and re-layouts: 7.74 us -> 2.74 us
    pallas_call x1, Pallas kernels: 56.2 us -> 41.5 us  [shards(): pl.pallas_call(functools.partial(kernel, n_wide, n_narrow), out_shape=(ja...]
    unnamed x16 -> x4, local copies, waits for them, and re-layouts: 7.74 us -> 2.74 us
where the time goes in v2:
time: 45.4 us; the launch traced here: 44.9 us
  Pallas kernels  41.5 us (91%)
  local copies, waits for them, and re-layouts  2.74 us (6%)
  between operations  0.65 us (1%)
    pallas_call x1, Pallas kernels, shards(): pl.pallas_call(functools.partial(kernel, n_wide, n_narrow), out_shape=(ja...  41.5 us
    unnamed x4, local copies, waits for them, and re-layouts  2.74 us

profile of v2, /device:TPU:1, one launch (start us, length us, event | category | flops | bytes accessed | tf_op | source)
XLA Modules:
  0.0 44.9 jit_solution(18029378566603387880)
XLA Ops:
  0.6 41.5 %shard_map.86 = (f32[16,64,128]{2,1,0:T(8,128)}, f32[128,8,128]{2,1,0:T(8,128)}) custom-call(f32[16,64,128]{2,1,0:T(8,128)} %sat_in.1, f32[16,64,128]{2,1,0:T(8,128)} %pres_in.1, s32[16,64,128]{2,1,0:T(8,128)} %rock_in.1, f32[3,16]{1,0:T(4,128)} %table_in.1, s32[64]{0:T(128)} %wcol_in.1, f32[64]{0:T(128)} %wrate_in.1, f32[128,8,128]{2,1,0:T(8,128)} %res_in.1), custom_call_target="tpu_custom_call" | custom-call | tf_op jit(solution)/shard_map/pallas_call | solution.py:513
  42.1 0.0 copy-start
  42.2 1.9 %copy.11 = f32[16,64,128]{2,1,0:T(8,128)} copy(f32[16,64,128]{2,1,0:T(8,128)} %get-tuple-element.4) | data formatting | bytes 1048576
  44.1 0.0 copy-done
  44.1 0.8 %copy.12 = f32[128,8,128]{2,1,0:T(8,128)} copy(f32[128,8,128]{2,1,0:T(8,128)S(1)} %copy-done) | data formatting | bytes 1048576
Async XLA Ops:
  42.1 2.0 %copy-start = (f32[128,8,128]{2,1,0:T(8,128)S(1)}, f32[128,8,128]{2,1,0:T(8,128)}, u32[]{:S(2)}) copy-start(f32[128,8,128]{2,1,0:T(8,128)} %get-tuple-element.5) | copy-start | bytes 1572868

commit v3 on v2

--- a/solution.py
+++ b/solution.py
@@ -37,12 +37,13 @@
 def kernel(
     n_wide, n_narrow,
     sat_in, pres_in, rock_in, table_in, wcol_in, wrate_in, res_in,
-    satnew_ref, prec_ref,
+    satnew_out, prec_out,
+    satnew_ref, prec_ref, outs,
     sat_ref, pres_ref, rock_ref, table_ref, wcol_ref, wrate_ref, res_ref,
     fields, gains, net, colpack, colhalo, colflow, source, maxw, maxn,
     slab, coef, dface, rface, cface, scale, first, va, vb,
     rowsend, rowhalo, rowterm, packs, packhalo, packterm, cw, cn, sidepack, sidehalo,
-    loads, sends, recvs,
+    loads, stores, sends, recvs,
 ):
     depth, rows, cols = sat_ref.shape
     layers, brick_rows, _ = res_ref.shape
@@ -184,9 +185,10 @@
         gains[d, 1] = oil
         for f, value in enumerate((pres_ref[d], perm, frac)):
             fields[d + 1, f] = value
-            turned = pltpu.roll(value, d + f * depth, 1)
-            packed_low = jnp.where(lane == d + f * depth, turned, packed_low)
-            packed_high = jnp.where(lane == lax.rem(d + f * depth + cols - 1, cols), turned, packed_high)
+            spot = 2 * (d + f * depth)
+            turned = pltpu.roll(value, spot, 1)
+            packed_low = jnp.where(lane == spot, turned, packed_low)
+            packed_high = jnp.where(lane == lax.rem(spot + cols - 1, cols), turned, packed_high)
         return packed_low, packed_high
 
     blank = jnp.ones((rows, cols), F32)
@@ -202,8 +204,81 @@
         "narrow", colpack.at[0], colpack.at[1], colhalo.at[0], colhalo.at[1]
     )
 
+    nothing = jnp.zeros((rows, cols), F32)
+    has_below, has_above = has["wide"]
+    has_left, has_right = has["narrow"]
+
+    def plane(d):
+        return [fields[d, f] for f in range(3)]
+
+    def transport(d, carry):
+        below_total, below_water = carry
+        here = plane(d + 1)
+        above_total, above_water = flows(here, plane(lax.min(d + 2, depth)), gravity)
+        above_total = jnp.where(d < depth - 1, above_total, nothing)
+        above_water = jnp.where(d < depth - 1, above_water, nothing)
+        flow = above_water - below_water
+        out = jnp.maximum(above_total, 0.0) + jnp.maximum(-below_total, 0.0)
+
+        total, water = flows(here, [pltpu.roll(x, rows - 1, 0) for x in here], 0.0)
+        total = jnp.where(row == rows - 1, 0.0, total)
+        water = jnp.where(row == rows - 1, 0.0, water)
+        flow = flow + (water - pltpu.roll(water, 1, 0))
+        out = out + (jnp.maximum(total, 0.0) + jnp.maximum(-pltpu.roll(total, 1, 0), 0.0))
+
+        total, water = flows(here, [pltpu.roll(x, cols - 1, 1) for x in here], 0.0)
+        total = jnp.where(lane == cols - 1, 0.0, total)
+        water = jnp.where(lane == cols - 1, 0.0, water)
+        net[d] = flow + (water - pltpu.roll(water, 1, 1))
+        outs[d] = out + (jnp.maximum(total, 0.0) + jnp.maximum(-pltpu.roll(total, 1, 1), 0.0))
+        return above_total, above_water
+
+    lax.fori_loop(0, depth, transport, (nothing, nothing))
+
+    wait_cols()
+
+    def unpack(block):
+        return [block] + [pltpu.roll(block, cols - 2 * f * depth, 1) for f in (1, 2)]
+
+    low_total, low_water = flows(unpack(colhalo[0]), unpack(colpack[0]), 0.0)
+    high_total, high_water = flows(unpack(colpack[1]), unpack(colhalo[1]), 0.0)
+    even = lax.rem(lane, 2) == 0
+    colflow[0] = jnp.where(
+        even,
+        jnp.where(has_right, high_water, nothing),
+        pltpu.roll(jnp.where(has_left, -low_water, nothing), 1, 1),
+    )
+    colflow[1] = jnp.maximum(jnp.where(
+        even,
+        jnp.where(has_right, high_total, nothing),
+        pltpu.roll(jnp.where(has_left, -low_total, nothing), 1, 1),
+    ), 0.0)
+
+    wait_planes()
+    side_total, side_water = flows(plane(0), plane(1), gravity)
+    net[0] = net[0] - jnp.where(has_below, side_water, nothing)
+    outs[0] = outs[0] + jnp.maximum(jnp.where(has_below, -side_total, nothing), 0.0)
+    side_total, side_water = flows(plane(depth), plane(depth + 1), gravity)
+    net[depth - 1] = net[depth - 1] + jnp.where(has_above, side_water, nothing)
+    outs[depth - 1] = outs[depth - 1] + jnp.maximum(jnp.where(has_above, side_total, nothing), 0.0)
+    edge = (lane == 0) | (lane == cols - 1)
+
+    def add_sides(i, most):
+        for u in range(2):
+            d = i * 2 + u
+            turn = cols - 1 - 2 * d
+            net[d] = net[d] + jnp.where(edge, pltpu.roll(colflow[0], turn, 1), 0.0)
+            most = jnp.maximum(
+                most, outs[d] + jnp.where(edge, pltpu.roll(colflow[1], turn, 1), 0.0)
+            )
+        return most
+
+    most = lax.fori_loop(0, depth // 2, add_sides, nothing)
+
+    maxw[w] = jnp.max(most.reshape(rows // brick_rows, brick_rows, cols), axis=0)
+    wait_wide = everyone("wide", lambda peer: maxw.at[w], lambda sender: maxw.at[sender])
+
     all_cols = cols * n_narrow
-
     for copy in loading[4:]:
         copy.wait()
     cell = row * cols + lane
@@ -217,68 +292,13 @@
             total = total + jnp.where(cell == target, wrate_ref[i * 8 + u], 0.0)
         return total
 
-    source[...] = lax.fori_loop(0, wcol_ref.shape[0] // 8, well, jnp.zeros((rows, cols), F32))
+    source[...] = lax.fori_loop(0, wcol_ref.shape[0] // 8, well, nothing)
 
     def add_res(i, total):
         return total + jnp.sum(res_ref[pl.ds(i * 16, 16)], axis=0)
 
     res_total = jnp.sum(lax.fori_loop(0, layers // 16, add_res, zero), axis=(0, 1), keepdims=True)
-
-    wait_cols()
-
-    def unpack(block):
-        return [block] + [pltpu.roll(block, cols - f * depth, 1) for f in (1, 2)]
-
-    low_total, low_water = flows(unpack(colhalo[0]), unpack(colpack[0]), 0.0)
-    high_total, high_water = flows(unpack(colpack[1]), unpack(colhalo[1]), 0.0)
-    has_left, has_right = has["narrow"]
-    nothing = jnp.zeros((rows, cols), F32)
-    colflow[0] = jnp.where(has_left, low_total, nothing)
-    colflow[1] = jnp.where(has_left, low_water, nothing)
-    colflow[2] = jnp.where(has_right, high_total, nothing)
-    colflow[3] = jnp.where(has_right, high_water, nothing)
-
-    wait_planes()
-    has_below, has_above = has["wide"]
-
-    def plane(d):
-        return [fields[d, f] for f in range(3)]
-
-    under_total, under_water = flows(plane(0), plane(1), gravity)
-    under_total = jnp.where(has_below, under_total, nothing)
-    under_water = jnp.where(has_below, under_water, nothing)
-
-    def transport(d, carry):
-        below_total, below_water, most = carry
-        here = plane(d + 1)
-        above_total, above_water = flows(here, plane(d + 2), gravity)
-        open_face = (d < depth - 1) | has_above
-        above_total = jnp.where(open_face, above_total, nothing)
-        above_water = jnp.where(open_face, above_water, nothing)
-        flow = above_water - below_water
-        out = jnp.maximum(above_total, 0.0) + jnp.maximum(-below_total, 0.0)
-
-        total, water = flows(here, [pltpu.roll(x, rows - 1, 0) for x in here], 0.0)
-        total = jnp.where(row == rows - 1, 0.0, total)
-        water = jnp.where(row == rows - 1, 0.0, water)
-        flow = flow + (water - pltpu.roll(water, 1, 0))
-        out = out + (jnp.maximum(total, 0.0) + jnp.maximum(-pltpu.roll(total, 1, 0), 0.0))
-
-        total, water = flows(here, [pltpu.roll(x, cols - 1, 1) for x in here], 0.0)
-        to_low = lax.rem(cols - d, cols)
-        low = [jnp.where(lane == 0, pltpu.roll(colflow[i], to_low, 1), pltpu.roll(x, 1, 1))
-               for i, x in ((0, total), (1, water))]
-        high = [jnp.where(lane == cols - 1, pltpu.roll(colflow[i], cols - 1 - d, 1), x)
-                for i, x in ((2, total), (3, water))]
-        flow = flow + (high[1] - low[1])
-        out = out + (jnp.maximum(high[0], 0.0) + jnp.maximum(-low[0], 0.0))
-        net[d] = flow
-        return above_total, above_water, jnp.maximum(most, out)
-
-    _, _, most = lax.fori_loop(0, depth, transport, (under_total, under_water, nothing))
-
-    maxw[w] = jnp.max(most.reshape(rows // brick_rows, brick_rows, cols), axis=0)
-    everyone("wide", lambda peer: maxw.at[w], lambda sender: maxw.at[sender])()
+    wait_wide()
     maxn[k] = jnp.max(maxw[...], axis=0)
     everyone("narrow", lambda peer: maxn.at[k], lambda sender: maxn.at[sender])()
     top_rate = jnp.max(jnp.max(maxn[...], axis=0), axis=(0, 1), keepdims=True)
@@ -301,6 +321,8 @@
     total, cross, packed_low, packed_high = lax.fori_loop(
         0, depth, update, (nothing, nothing, blank, blank)
     )
+    storing = pltpu.make_async_copy(satnew_ref, satnew_out, loads.at[0])
+    storing.start()
     sidepack[0] = packed_low
     sidepack[1] = pltpu.roll(packed_high, 1, 1)
     wait_sides = neighbours(
@@ -437,12 +459,23 @@
         for i, away in ((2, -1), (3, 1), (4, -n_wide), (5, n_wide)):
             matrix = jnp.where(blane == brow + away, matrix - gathered[:, i:i + 1], matrix)
         right = jnp.broadcast_to(gathered[:, 0:1], (bricks, cols))
+        def pivoted(j, block, side):
+            column = jnp.broadcast_to(block[:, j:j + 1], (bricks, cols))
+            factor = jnp.where(brow == j, 0.0, column / column[j:j + 1])
+            return factor * block[j:j + 1], factor * side[j:j + 1]
+
+        def colour(j):
+            return (j // n_wide + j % n_wide) % 2
+
+        block, side = matrix, right
         for j in range(bricks):
-            column = jnp.broadcast_to(matrix[:, j:j + 1], (bricks, cols))
-            factor = jnp.where(brow == j, 0.0, column / column[j:j + 1])
-            matrix, right = (
-                matrix - factor * matrix[j:j + 1], right - factor * right[j:j + 1]
-            )
+            if colour(j) == 0:
+                change, side_change = pivoted(j, block, side)
+                matrix, right = matrix - change, right - side_change
+        for j in range(bricks):
+            if colour(j) == 1:
+                change, side_change = pivoted(j, matrix, right)
+                matrix, right = matrix - change, right - side_change
         own = brow == mine
         pivot = jnp.sum(jnp.where(own & (blane == mine), matrix, 0.0), axis=(0, 1), keepdims=True)
         answer = jnp.sum(jnp.where(own & (blane == 0), right, 0.0), axis=(0, 1), keepdims=True)
@@ -468,6 +501,10 @@
         c = jnp.where(present, packhalo[side, 0], 0.0)
         packterm[side, 0] = c
         packterm[side, 1] = jnp.where(present, c * packhalo[side, 1], 0.0)
+
+    def store(i):
+        part = pl.ds(i * unroll, unroll)
+        return pltpu.make_async_copy(prec_ref.at[part], prec_out.at[part], stores.at[i])
 
     for t in range(tiles):
         tile = pl.ds(t * brick_rows, brick_rows)
@@ -490,9 +527,26 @@
                         + jnp.where(tlane == cols - 1, right, 0.0)
                     )
                 prec_ref[layer] = sums[1] / sums[0] + coarse_value
+            store(t * (cols // unroll) + i).start()
             return carry
 
         lax.fori_loop(0, cols // unroll, average, 0)
+
+    storing.wait()
+    for i in range(layers // unroll):
+        store(i).wait()
+
+
+def deliver(a_in, b_in, a_out, b_out, sems):
+    copies = []
+    for src, dst in ((a_in, a_out), (b_in, b_out)):
+        part = src.shape[0] // 4
+        for i in range(4):
+            at = pl.ds(i * part, part)
+            copies.append(pltpu.make_async_copy(src.at[at], dst.at[at], sems.at[len(copies)]))
+            copies[-1].start()
+    for copy in copies:
+        copy.wait()
 
 
 def shards(n_wide, n_narrow, *args):
@@ -503,22 +557,24 @@
     bricks = n_wide * n_narrow
     cells = layers * brick_rows
     copies = 2 * 7 + 3 * (n_wide - 1) + 2 * (n_narrow - 1)
-    vmem = pl.BlockSpec(memory_space=pltpu.VMEM)
     anywhere = pl.BlockSpec(memory_space=pl.ANY)
     table, wells = args[3].shape, args[4].shape
 
     def buffer(*shape):
         return pltpu.VMEM(shape, F32)
 
-    return pl.pallas_call(
+    outputs = pl.pallas_call(
         functools.partial(kernel, n_wide, n_narrow),
         out_shape=(
             jax.ShapeDtypeStruct(sat.shape, F32),
             jax.ShapeDtypeStruct(residual.shape, F32),
         ),
         in_specs=[anywhere] * 7,
-        out_specs=(vmem, vmem),
+        out_specs=(anywhere, anywhere),
         scratch_shapes=[
+            buffer(*sat.shape),
+            buffer(*residual.shape),
+            buffer(*sat.shape),
             buffer(*sat.shape),
             buffer(*sat.shape),
             pltpu.VMEM(sat.shape, jnp.int32),
@@ -531,7 +587,7 @@
             buffer(depth, rows, cols),
             buffer(2, rows, cols),
             buffer(2, rows, cols),
-            buffer(4, rows, cols),
+            buffer(2, rows, cols),
             buffer(rows, cols),
             buffer(n_wide, brick_rows, cols),
             buffer(n_narrow, brick_rows, cols),
@@ -555,6 +611,7 @@
             buffer(2, rows, cols),
             buffer(2, rows, cols),
             pltpu.SemaphoreType.DMA((7,)),
+            pltpu.SemaphoreType.DMA((layers // 16,)),
             pltpu.SemaphoreType.DMA((copies,)),
             pltpu.SemaphoreType.DMA((copies,)),
         ],
@@ -562,6 +619,17 @@
             collective_id=0, has_side_effects=True, vmem_limit_bytes=56 * 1024 * 1024
         ),
     )(*args)
+    return pl.pallas_call(
+        deliver,
+        out_shape=(
+            jax.ShapeDtypeStruct(sat.shape, F32),
+            jax.ShapeDtypeStruct(residual.shape, F32),
+        ),
+        in_specs=[anywhere] * 2,
+        out_specs=(anywhere, anywhere),
+        scratch_shapes=[pltpu.SemaphoreType.DMA((8,))],
+        compiler_params=pltpu.CompilerParams(vmem_limit_bytes=60 * 1024 * 1024),
+    )(*outputs)
 
 
 def solution(mesh):

time: 45.4 us -> 71.6 us (1.58)
  Pallas kernels: 41.5 us -> 70.8 us
  local copies, waits for them, and re-layouts: 2.74 us -> 0 us
    pallas_call x0 -> x1, Pallas kernels: none -> 32.9 us  [shards(): pl.pallas_call(deliver, out_shape=(jax.ShapeDtypeStruct(sat.shape, F32),...]
    pallas_call x1, Pallas kernels: 41.5 us -> 37.9 us  [shards(): pl.pallas_call(functools.partial(kernel, n_wide, n_narrow), out_shape=(ja...]
    unnamed x4 -> x0, local copies, waits for them, and re-layouts: 2.74 us -> none
where the time goes in v3:
time: 71.6 us; the launch traced here: 71.5 us
  Pallas kernels  70.8 us (99%)
    pallas_call x1, Pallas kernels, shards(): pl.pallas_call(functools.partial(kernel, n_wide, n_narrow), out_shape=(ja...  37.9 us
    pallas_call x1, Pallas kernels, shards(): pl.pallas_call(deliver, out_shape=(jax.ShapeDtypeStruct(sat.shape, F32),...  32.9 us

profile of v3, /device:TPU:1, one launch (start us, length us, event | category | flops | bytes accessed | tf_op | source)
XLA Modules:
  0.0 71.5 jit_solution(10071941582469994014)
XLA Ops:
  0.6 37.9 %shard_map.86 = (f32[16,64,128]{2,1,0:T(8,128)}, f32[128,8,128]{2,1,0:T(8,128)}) custom-call(f32[16,64,128]{2,1,0:T(8,128)} %sat_in.1, f32[16,64,128]{2,1,0:T(8,128)} %pres_in.1, s32[16,64,128]{2,1,0:T(8,128)} %rock_in.1, f32[3,16]{1,0:T(4,128)} %table_in.1, s32[64]{0:T(128)} %wcol_in.1, f32[64]{0:T(128)} %wrate_in.1, f32[128,8,128]{2,1,0:T(8,128)} %res_in.1), custom_call_target="tpu_custom_call" | custom-call | tf_op jit(solution)/shard_map/pallas_call | solution.py:566
  38.5 32.9 %shard_map.87 = (f32[16,64,128]{2,1,0:T(8,128)}, f32[128,8,128]{2,1,0:T(8,128)}) custom-call(f32[16,64,128]{2,1,0:T(8,128)} %get-tuple-element.4.a_in, f32[128,8,128]{2,1,0:T(8,128)} %get-tuple-element.5.b_in), custom_call_target="tpu_custom_call" | custom-call | tf_op jit(solution)/shard_map/pallas_call | solution.py:622

commit v4 on v3

--- a/solution.py
+++ b/solution.py
@@ -332,8 +332,45 @@
     def part(sender):
         return coef.at[pl.ds(pl.multiple_of(sender * band, band), band), :]
 
-    wait_bricks = everyone("wide", lambda peer: slab.at[peer], part)
+    bulk = count[0]
+
+    def brick_copy(number, sender, peer):
+        return remote(slab.at[peer], part(sender), bulk + number, "wide", peer)
+
+    for off in range(1, n_wide):
+        slot()
+        brick_copy(off - 1, w, lax.rem(w + off, n_wide)).start()
+
+    last_row = brick_rows - 1
+    packs[...] = jnp.zeros(packs.shape, F32)
+
+    def at_layer(z):
+        return pl.ds(pl.multiple_of(z * brick_rows, brick_rows), brick_rows)
+
+    def assemble_band(band_number):
+        base = band_number * depth
+        lane_base = lax.rem(base, cols)
+        tile = at_layer(lax.div(base, cols))
+        low = packs[0, 0, tile, :]
+        high = packs[1, 0, tile, :]
+        for u in range(depth):
+            here = coef[at_layer(base + u), :]
+            rf = jnp.where(trow == last_row, 0.0, harmonic(here, pltpu.roll(here, last_row, 0)))
+            cf = jnp.where(tlane == cols - 1, 0.0, harmonic(here, pltpu.roll(here, cols - 1, 1)))
+            rface[at_layer(base + u), :] = rf
+            cface[at_layer(base + u), :] = cf
+            scale[at_layer(base + u), :] = (
+                compress * here + pltpu.roll(rf, 1, 0) + rf + pltpu.roll(cf, 1, 1) + cf
+            )
+            spot = lane_base + u
+            turned = pltpu.roll(here, spot, 1)
+            low = jnp.where(tlane == spot, turned, low)
+            high = jnp.where(tlane == lax.rem(spot + cols - 1, cols), turned, high)
+        packs[0, 0, tile, :] = low
+        packs[1, 0, tile, :] = high
+
     coef[pl.ds(pl.multiple_of(w * band, band), band), :] = slab[w]
+    assemble_band(w)
 
     brick_count = n_wide
 
@@ -356,16 +393,24 @@
     for i, value in enumerate((diagonal, low_rows, high_rows, low_cols, high_cols)):
         message = jnp.where(clane == i + 1, value, message)
     cw[w] = message
-    everyone("wide", lambda peer: cw.at[w], lambda sender: cw.at[sender])()
+    wait_sums = everyone("wide", lambda peer: cw.at[w], lambda sender: cw.at[sender])
+
+    def take_band(off, carry):
+        sender = lax.rem(w + n_wide - off, n_wide)
+        brick_copy(off - 1, sender, sender).wait_recv()
+        assemble_band(sender)
+        return carry
+
+    lax.fori_loop(1, n_wide, take_band, 0)
+    wait_sums()
 
     def at_narrow(sender):
         return cn.at[pl.ds(pl.multiple_of(sender * n_wide, n_wide), n_wide), :]
 
     cn[pl.ds(pl.multiple_of(k * n_wide, n_wide), n_wide), :] = jnp.sum(cw[...], axis=0)
     wait_coarse = everyone("narrow", lambda peer: at_narrow(k), at_narrow)
-    wait_bricks()
-
-    last_row = brick_rows - 1
+    for off in range(1, n_wide):
+        brick_copy(off - 1, w, lax.rem(w + off, n_wide)).wait_send()
 
     def send_sides(ref, which):
         rowsend[0, which] = ref[pl.ds(0, layers, stride=brick_rows), :]
@@ -375,6 +420,9 @@
             rowhalo.at[0, which], rowhalo.at[1, which],
         )
         for t in range(tiles):
+            if which == 0:
+                break
+
             def collect(i, carry):
                 low, high = carry
                 for u in range(32):
@@ -387,7 +435,8 @@
 
             low, high = lax.fori_loop(0, cols // 32, collect, (zero, zero))
             packs[0, which, pl.ds(t * brick_rows, brick_rows), :] = low
-            packs[1, which, pl.ds(t * brick_rows, brick_rows), :] = pltpu.roll(high, 1, 1)
+            packs[1, which, pl.ds(t * brick_rows, brick_rows), :] = high
+        packs[1, which] = pltpu.roll(packs[1, which], 1, 1)
         wait_packs = neighbours(
             "narrow", packs.at[0, which], packs.at[1, which],
             packhalo.at[0, which], packhalo.at[1, which],
@@ -398,24 +447,14 @@
 
     unroll = 16
 
-    def at_layer(z):
-        return pl.ds(pl.multiple_of(z * brick_rows, brick_rows), brick_rows)
-
     def assemble(i, carry):
         below, here = carry
-        for u in range(unroll):
-            z = i * unroll + u
+        for u in range(32):
+            z = i * 32 + u
             above = coef[at_layer(z + 1), :]
             df = jnp.where(z < layers - 1, harmonic(here, above), zero)
-            rf = jnp.where(trow == last_row, 0.0, harmonic(here, pltpu.roll(here, last_row, 0)))
-            cf = jnp.where(tlane == cols - 1, 0.0, harmonic(here, pltpu.roll(here, cols - 1, 1)))
-            diag = (
-                compress * here + below + df + pltpu.roll(rf, 1, 0) + rf + pltpu.roll(cf, 1, 1) + cf
-            )
-            sc = relax / diag
+            sc = relax / (scale[at_layer(z), :] + below + df)
             dface[at_layer(z), :] = df
-            rface[at_layer(z), :] = rf
-            cface[at_layer(z), :] = cf
             scale[at_layer(z), :] = sc
             v = sc * res_ref[z]
             first[at_layer(z), :] = v
@@ -423,7 +462,7 @@
             below, here = df, above
         return below, here
 
-    lax.fori_loop(0, layers // unroll, assemble, (zero, coef[pl.ds(0, brick_rows), :]))
+    lax.fori_loop(0, layers // 32, assemble, (zero, coef[pl.ds(0, brick_rows), :]))
 
     def sweep(src, dst):
         def body(i, carry):
@@ -537,16 +576,21 @@
         store(i).wait()
 
 
-def deliver(a_in, b_in, a_out, b_out, sems):
-    copies = []
-    for src, dst in ((a_in, a_out), (b_in, b_out)):
+def deliver(a_in, b_in, a_out, b_out, a_held, b_held, arrive, leave):
+    arriving, leaving = [], []
+    for src, held, dst in ((a_in, a_held, a_out), (b_in, b_held, b_out)):
         part = src.shape[0] // 4
         for i in range(4):
             at = pl.ds(i * part, part)
-            copies.append(pltpu.make_async_copy(src.at[at], dst.at[at], sems.at[len(copies)]))
-            copies[-1].start()
-    for copy in copies:
-        copy.wait()
+            number = len(arriving)
+            arriving.append(pltpu.make_async_copy(src.at[at], held.at[at], arrive.at[number]))
+            leaving.append(pltpu.make_async_copy(held.at[at], dst.at[at], leave.at[number]))
+            arriving[-1].start()
+    for first, second in zip(arriving, leaving):
+        first.wait()
+        second.start()
+    for second in leaving:
+        second.wait()
 
 
 def shards(n_wide, n_narrow, *args):
@@ -627,7 +671,12 @@
         ),
         in_specs=[anywhere] * 2,
         out_specs=(anywhere, anywhere),
-        scratch_shapes=[pltpu.SemaphoreType.DMA((8,))],
+        scratch_shapes=[
+            buffer(*sat.shape),
+            buffer(*residual.shape),
+            pltpu.SemaphoreType.DMA((8,)),
+            pltpu.SemaphoreType.DMA((8,)),
+        ],
         compiler_params=pltpu.CompilerParams(vmem_limit_bytes=60 * 1024 * 1024),
     )(*outputs)
 

time: 71.6 us -> 39.3 us (0.55)
  Pallas kernels: 70.8 us -> 38.5 us
    pallas_call x1, Pallas kernels: 32.9 us -> 2.09 us  [shards(): pl.pallas_call(deliver, out_shape=(jax.ShapeDtypeStruct(sat.shape, F32),...]
    pallas_call x1, Pallas kernels: 37.9 us -> 36.4 us  [shards(): pl.pallas_call(functools.partial(kernel, n_wide, n_narrow), out_shape=(ja...]
where the time goes in v4:
time: 39.3 us; the launch traced here: 39.1 us
  Pallas kernels  38.5 us (98%)
  between operations  0.64 us (2%)
    pallas_call x1, Pallas kernels, shards(): pl.pallas_call(functools.partial(kernel, n_wide, n_narrow), out_shape=(ja...  36.4 us
    pallas_call x1, Pallas kernels, shards(): pl.pallas_call(deliver, out_shape=(jax.ShapeDtypeStruct(sat.shape, F32),...  2.09 us

profile of v4, /device:TPU:1, one launch (start us, length us, event | category | flops | bytes accessed | tf_op | source)
XLA Modules:
  0.0 39.1 jit_solution(275106747406604604)
XLA Ops:
  0.6 36.4 %shard_map.86 = (f32[16,64,128]{2,1,0:T(8,128)}, f32[128,8,128]{2,1,0:T(8,128)}) custom-call(f32[16,64,128]{2,1,0:T(8,128)} %sat_in.1, f32[16,64,128]{2,1,0:T(8,128)} %pres_in.1, s32[16,64,128]{2,1,0:T(8,128)} %rock_in.1, f32[3,16]{1,0:T(4,128)} %table_in.1, s32[64]{0:T(128)} %wcol_in.1, f32[64]{0:T(128)} %wrate_in.1, f32[128,8,128]{2,1,0:T(8,128)} %res_in.1), custom_call_target="tpu_custom_call" | custom-call | tf_op jit(solution)/shard_map/pallas_call | solution.py:610
  37.0 2.1 %shard_map.87 = (f32[16,64,128]{2,1,0:T(8,128)}, f32[128,8,128]{2,1,0:T(8,128)}) custom-call(f32[16,64,128]{2,1,0:T(8,128)} %get-tuple-element.4.a_in, f32[128,8,128]{2,1,0:T(8,128)} %get-tuple-element.5.b_in), custom_call_target="tpu_custom_call" | custom-call | tf_op jit(solution)/shard_map/pallas_call | solution.py:666

commit v5 on v4

--- a/solution.py
+++ b/solution.py
@@ -41,7 +41,7 @@
     satnew_ref, prec_ref, outs,
     sat_ref, pres_ref, rock_ref, table_ref, wcol_ref, wrate_ref, res_ref,
     fields, gains, net, colpack, colhalo, colflow, source, maxw, maxn,
-    slab, coef, dface, rface, cface, scale, first, va, vb,
+    slab, coef, dface, rface, cface, scale, first, va,
     rowsend, rowhalo, rowterm, packs, packhalo, packterm, cw, cn, sidepack, sidehalo,
     loads, stores, sends, recvs,
 ):
@@ -160,7 +160,6 @@
 
     coef[pl.ds(layers * brick_rows, brick_rows), :] = one
     va[pl.ds(layers * brick_rows, brick_rows), :] = zero
-    vb[pl.ds(layers * brick_rows, brick_rows), :] = zero
 
     rocks = table_ref.shape[1]
     for copy in loading[:4]:
@@ -211,8 +210,7 @@
     def plane(d):
         return [fields[d, f] for f in range(3)]
 
-    def transport(d, carry):
-        below_total, below_water = carry
+    def transport(d, below_total, below_water):
         here = plane(d + 1)
         above_total, above_water = flows(here, plane(lax.min(d + 2, depth)), gravity)
         above_total = jnp.where(d < depth - 1, above_total, nothing)
@@ -233,7 +231,12 @@
         outs[d] = out + (jnp.maximum(total, 0.0) + jnp.maximum(-pltpu.roll(total, 1, 1), 0.0))
         return above_total, above_water
 
-    lax.fori_loop(0, depth, transport, (nothing, nothing))
+    def transport_group(i, carry):
+        for u in range(4):
+            carry = transport(i * 4 + u, *carry)
+        return carry
+
+    lax.fori_loop(0, depth // 4, transport_group, (nothing, nothing))
 
     wait_cols()
 
@@ -304,42 +307,54 @@
     top_rate = jnp.max(jnp.max(maxn[...], axis=0), axis=(0, 1), keepdims=True)
     step_size = courant / (top_rate + tiny)
 
-    def update(d, carry):
-        total, cross, packed_low, packed_high = carry
-        s = sat_ref[d] - step_size * net[d] + step_size * source[...]
-        satnew_ref[d] = s
-        value = fields[d + 1, 1] * (gains[d, 0] * s * s + gains[d, 1] * (1.0 - s) * (1.0 - s))
-        at = pl.multiple_of(d * brick_rows, brick_rows)
-        for p in range(n_wide):
-            slab[p, pl.ds(at, brick_rows), :] = value[p * brick_rows:(p + 1) * brick_rows]
-        turned = pltpu.roll(value, d, 1)
-        packed_low = jnp.where(lane == d, turned, packed_low)
-        packed_high = jnp.where(lane == lax.rem(d + cols - 1, cols), turned, packed_high)
-        cross = cross + harmonic(value, pltpu.roll(value, rows - 1, 0))
-        return total + value, cross, packed_low, packed_high
-
-    total, cross, packed_low, packed_high = lax.fori_loop(
-        0, depth, update, (nothing, nothing, blank, blank)
-    )
+    def update(i, carry):
+        for u in range(2):
+            d = i * 2 + u
+            s = sat_ref[d] - step_size * net[d] + step_size * source[...]
+            satnew_ref[d] = s
+            value = fields[d + 1, 1] * (gains[d, 0] * s * s + gains[d, 1] * (1.0 - s) * (1.0 - s))
+            at = pl.multiple_of(d * brick_rows, brick_rows)
+            for p in range(n_wide):
+                slab[p, pl.ds(at, brick_rows), :] = value[p * brick_rows:(p + 1) * brick_rows]
+        return carry
+
+    lax.fori_loop(0, depth // 2, update, 0)
+
+    def part(sender):
+        return coef.at[pl.ds(pl.multiple_of(sender * band, band), band), :]
+
+    bulk = count[0]
+
+    def brick_copy(number, sender, peer):
+        return remote(slab.at[peer], part(sender), bulk + number, "wide", peer)
+
+    for off in range(1, n_wide):
+        slot()
+        brick_copy(off - 1, w, lax.rem(w + off, n_wide)).start()
     storing = pltpu.make_async_copy(satnew_ref, satnew_out, loads.at[0])
     storing.start()
+
+    def survey(i, carry):
+        total, cross, packed_low, packed_high = carry
+        for u in range(2):
+            d = i * 2 + u
+            at = pl.ds(pl.multiple_of(d * brick_rows, brick_rows), brick_rows)
+            value = jnp.concatenate([slab[p, at, :] for p in range(n_wide)], axis=0)
+            turned = pltpu.roll(value, d, 1)
+            packed_low = jnp.where(lane == d, turned, packed_low)
+            packed_high = jnp.where(lane == lax.rem(d + cols - 1, cols), turned, packed_high)
+            cross = cross + harmonic(value, pltpu.roll(value, rows - 1, 0))
+            total = total + value
+        return total, cross, packed_low, packed_high
+
+    total, cross, packed_low, packed_high = lax.fori_loop(
+        0, depth // 2, survey, (nothing, nothing, blank, blank)
+    )
     sidepack[0] = packed_low
     sidepack[1] = pltpu.roll(packed_high, 1, 1)
     wait_sides = neighbours(
         "narrow", sidepack.at[0], sidepack.at[1], sidehalo.at[0], sidehalo.at[1]
     )
-
-    def part(sender):
-        return coef.at[pl.ds(pl.multiple_of(sender * band, band), band), :]
-
-    bulk = count[0]
-
-    def brick_copy(number, sender, peer):
-        return remote(slab.at[peer], part(sender), bulk + number, "wide", peer)
-
-    for off in range(1, n_wide):
-        slot()
-        brick_copy(off - 1, w, lax.rem(w + off, n_wide)).start()
 
     last_row = brick_rows - 1
     packs[...] = jnp.zeros(packs.shape, F32)
@@ -419,23 +434,6 @@
             "wide", rowsend.at[0, which], rowsend.at[1, which],
             rowhalo.at[0, which], rowhalo.at[1, which],
         )
-        for t in range(tiles):
-            if which == 0:
-                break
-
-            def collect(i, carry):
-                low, high = carry
-                for u in range(32):
-                    z = i * 32 + u
-                    at = pl.multiple_of((t * cols + z) * brick_rows, brick_rows)
-                    turned = pltpu.roll(ref[pl.ds(at, brick_rows), :], z, 1)
-                    low = jnp.where(tlane == z, turned, low)
-                    high = jnp.where(tlane == lax.rem(z + cols - 1, cols), turned, high)
-                return low, high
-
-            low, high = lax.fori_loop(0, cols // 32, collect, (zero, zero))
-            packs[0, which, pl.ds(t * brick_rows, brick_rows), :] = low
-            packs[1, which, pl.ds(t * brick_rows, brick_rows), :] = high
         packs[1, which] = pltpu.roll(packs[1, which], 1, 1)
         wait_packs = neighbours(
             "narrow", packs.at[0, which], packs.at[1, which],
@@ -445,7 +443,7 @@
 
     wait_rows, wait_packs = send_sides(coef, 0)
 
-    unroll = 16
+    unroll = 32
 
     def assemble(i, carry):
         below, here = carry
@@ -464,12 +462,14 @@
 
     lax.fori_loop(0, layers // 32, assemble, (zero, coef[pl.ds(0, brick_rows), :]))
 
-    def sweep(src, dst):
+    group = min(64, layers)
+
+    def sweep(packing):
         def body(i, carry):
-            v_below, d_below, v = carry
-            for u in range(32):
-                z = i * 32 + u
-                v_above = src[at_layer(z + 1), :]
+            v_below, d_below, v, low, high = carry
+            for u in range(group):
+                z = i * group + u
+                v_above = va[at_layer(z + 1), :]
                 df = dface[at_layer(z), :]
                 rf = rface[at_layer(z), :]
                 cf = cface[at_layer(z), :]
@@ -478,13 +478,21 @@
                     + pltpu.roll(rf * v, 1, 0) + rf * pltpu.roll(v, last_row, 0)
                     + pltpu.roll(cf * v, 1, 1) + cf * pltpu.roll(v, cols - 1, 1)
                 )
-                dst[at_layer(z), :] = (
-                    (1.0 - relax) * v + first[at_layer(z), :] + scale[at_layer(z), :] * off
-                )
+                fresh = (1.0 - relax) * v + first[at_layer(z), :] + scale[at_layer(z), :] * off
+                va[at_layer(z), :] = fresh
+                if packing:
+                    spot = lax.rem(z, cols)
+                    turned = pltpu.roll(fresh, spot, 1)
+                    low = jnp.where(tlane == spot, turned, low)
+                    high = jnp.where(tlane == lax.rem(spot + cols - 1, cols), turned, high)
                 v_below, d_below, v = v, df, v_above
-            return v_below, d_below, v
-
-        lax.fori_loop(0, layers // 32, body, (zero, zero, src[pl.ds(0, brick_rows), :]))
+            if packing:
+                tile = at_layer(lax.div(i * group, cols))
+                packs[0, 1, tile, :] = low
+                packs[1, 1, tile, :] = high
+            return v_below, d_below, v, low, high
+
+        lax.fori_loop(0, layers // group, body, (zero, zero, va[pl.ds(0, brick_rows), :], zero, zero))
 
     bricks = n_wide * n_narrow
     blane = lax.broadcasted_iota(jnp.int32, (bricks, cols), 1)
@@ -520,11 +528,13 @@
         answer = jnp.sum(jnp.where(own & (blane == 0), right, 0.0), axis=(0, 1), keepdims=True)
         return answer / pivot
 
-    src, dst = va, vb
-    for number in range(SWEEPS - 1):
-        sweep(src, dst)
-        src, dst = dst, src
-    wait_value_rows, wait_value_packs = send_sides(src, 1)
+    def plain_sweep(number, carry):
+        sweep(False)
+        return carry
+
+    lax.fori_loop(0, SWEEPS - 2, plain_sweep, 0)
+    sweep(True)
+    wait_value_rows, wait_value_packs = send_sides(va, 1)
     wait_coarse()
     coarse_value = coarse_solve()
 
@@ -553,7 +563,7 @@
                 z = i * unroll + u
                 layer = t * cols + z
                 c = coef[at_layer(layer), :]
-                sums = [c, c * src[at_layer(layer), :]]
+                sums = [c, c * va[at_layer(layer), :]]
                 for j in range(2):
                     low = rowterm[0, j, pl.ds(layer, 1), :]
                     high = rowterm[1, j, pl.ds(layer, 1), :]
@@ -643,7 +653,6 @@
             buffer(cells, cols),
             buffer(cells, cols),
             buffer(cells + brick_rows, cols),
-            buffer(cells + brick_rows, cols),
             buffer(2, 2, layers, cols),
             buffer(2, 2, layers, cols),
             buffer(2, 2, layers, cols),
@@ -655,7 +664,7 @@
             buffer(2, rows, cols),
             buffer(2, rows, cols),
             pltpu.SemaphoreType.DMA((7,)),
-            pltpu.SemaphoreType.DMA((layers // 16,)),
+            pltpu.SemaphoreType.DMA((layers // 32,)),
             pltpu.SemaphoreType.DMA((copies,)),
             pltpu.SemaphoreType.DMA((copies,)),
         ],

time: 39.3 us -> 38.8 us (0.987)
  Pallas kernels: 38.5 us -> 38 us
    pallas_call x1, Pallas kernels: 36.4 us -> 36 us  [shards(): pl.pallas_call(functools.partial(kernel, n_wide, n_narrow), out_shape=(ja...]
where the time goes in v5:
time: 38.8 us; the launch traced here: 38.7 us
  Pallas kernels  38 us (98%)
  between operations  0.64 us (2%)
    pallas_call x1, Pallas kernels, shards(): pl.pallas_call(functools.partial(kernel, n_wide, n_narrow), out_shape=(ja...  36 us
    pallas_call x1, Pallas kernels, shards(): pl.pallas_call(deliver, out_shape=(jax.ShapeDtypeStruct(sat.shape, F32),...  2.09 us

profile of v5, /device:TPU:1, one launch (start us, length us, event | category | flops | bytes accessed | tf_op | source)
XLA Modules:
  0.0 38.7 jit_solution(13845793939211447592)
XLA Ops:
  0.6 36.0 %shard_map.86 = (f32[16,64,128]{2,1,0:T(8,128)}, f32[128,8,128]{2,1,0:T(8,128)}) custom-call(f32[16,64,128]{2,1,0:T(8,128)} %sat_in.1, f32[16,64,128]{2,1,0:T(8,128)} %pres_in.1, s32[16,64,128]{2,1,0:T(8,128)} %rock_in.1, f32[3,16]{1,0:T(4,128)} %table_in.1, s32[64]{0:T(128)} %wcol_in.1, f32[64]{0:T(128)} %wrate_in.1, f32[128,8,128]{2,1,0:T(8,128)} %res_in.1), custom_call_target="tpu_custom_call" | custom-call | tf_op jit(solution)/shard_map/pallas_call | solution.py:620
  36.6 2.1 %shard_map.87 = (f32[16,64,128]{2,1,0:T(8,128)}, f32[128,8,128]{2,1,0:T(8,128)}) custom-call(f32[16,64,128]{2,1,0:T(8,128)} %get-tuple-element.4.a_in, f32[128,8,128]{2,1,0:T(8,128)} %get-tuple-element.5.b_in), custom_call_target="tpu_custom_call" | custom-call | tf_op jit(solution)/shard_map/pallas_call | solution.py:675

commit v6 on v5

--- a/solution.py
+++ b/solution.py
@@ -43,6 +43,7 @@
     fields, gains, net, colpack, colhalo, colflow, source, maxw, maxn,
     slab, coef, dface, rface, cface, scale, first, va,
     rowsend, rowhalo, rowterm, packs, packhalo, packterm, cw, cn, sidepack, sidehalo,
+    sathalo, preshalo, rockhalo, satb, rockb, netb,
     loads, stores, sends, recvs,
 ):
     depth, rows, cols = sat_ref.shape
@@ -161,25 +162,60 @@
     coef[pl.ds(layers * brick_rows, brick_rows), :] = one
     va[pl.ds(layers * brick_rows, brick_rows), :] = zero
 
+    pl.semaphore_wait(barrier, n_wide + n_narrow - 2)
+
+    wait_raw = [
+        neighbours("wide", src.at[0], src.at[depth - 1], halo.at[0], halo.at[1])
+        for src, halo in ((sat_in, sathalo), (pres_in, preshalo), (rock_in, rockhalo))
+    ]
+
+    def brick_part(ref, sender):
+        return ref.at[pl.ds(pl.multiple_of(sender * depth, depth), depth)]
+
+    def brick_rows_of(ref, peer):
+        return ref.at[:, pl.ds(pl.multiple_of(peer * brick_rows, brick_rows), brick_rows), :]
+
+    raw = count[0]
+    raw_fields = ((sat_in, satb), (rock_in, rockb))
+
+    def raw_copy(off, f, sender, peer):
+        src, dst = raw_fields[f]
+        return remote(
+            brick_rows_of(src, peer), brick_part(dst, sender), raw + 2 * (off - 1) + f, "wide", peer
+        )
+
+    for off in range(1, n_wide):
+        for f in range(2):
+            slot()
+            raw_copy(off, f, w, lax.rem(w + off, n_wide)).start()
+    own_raw = [
+        pltpu.make_async_copy(brick_rows_of(src, w), brick_part(dst, w), loads.at[7 + f])
+        for f, (src, dst) in enumerate(raw_fields)
+    ]
+    for copy in own_raw:
+        copy.start()
+
     rocks = table_ref.shape[1]
     for copy in loading[:4]:
         copy.wait()
 
-    def derive(d, carry):
-        packed_low, packed_high = carry
-        rock = rock_ref[d]
+    def properties(rock):
         bits = []
         step = 1
         while step < rocks:
             bits.append((rock & step) != 0)
             step *= 2
-        perm = lookup(bits, table_ref, 0, rocks)
-        water = lookup(bits, table_ref, 1, rocks)
-        oil = lookup(bits, table_ref, 2, rocks)
-        s = sat_ref[d]
+        return [lookup(bits, table_ref, i, rocks) for i in range(3)]
+
+    def fraction(water, oil, s):
         water_mob = water * s * s
         oil_mob = oil * (1.0 - s) * (1.0 - s)
-        frac = water_mob / (water_mob + oil_mob)
+        return water_mob / (water_mob + oil_mob)
+
+    def derive(d, carry):
+        packed_low, packed_high = carry
+        perm, water, oil = properties(rock_ref[d])
+        frac = fraction(water, oil, sat_ref[d])
         gains[d, 0] = water
         gains[d, 1] = oil
         for f, value in enumerate((pres_ref[d], perm, frac)):
@@ -194,11 +230,6 @@
     packed_low, packed_high = lax.fori_loop(0, depth, derive, (blank, blank))
     colpack[0] = packed_low
     colpack[1] = pltpu.roll(packed_high, 1, 1)
-
-    pl.semaphore_wait(barrier, n_wide + n_narrow - 2)
-    wait_planes = neighbours(
-        "wide", fields.at[1], fields.at[depth], fields.at[0], fields.at[depth + 1]
-    )
     wait_cols = neighbours(
         "narrow", colpack.at[0], colpack.at[1], colhalo.at[0], colhalo.at[1]
     )
@@ -257,7 +288,16 @@
         pltpu.roll(jnp.where(has_left, -low_total, nothing), 1, 1),
     ), 0.0)
 
-    wait_planes()
+    for wait in wait_raw:
+        wait()
+    for side, at, present in ((0, 0, has_below), (1, depth + 1, has_above)):
+        @pl.when(present)
+        def _():
+            perm, water, oil = properties(rockhalo[side])
+            fields[at, 0] = preshalo[side]
+            fields[at, 1] = perm
+            fields[at, 2] = fraction(water, oil, sathalo[side])
+
     side_total, side_water = flows(plane(0), plane(1), gravity)
     net[0] = net[0] - jnp.where(has_below, side_water, nothing)
     outs[0] = outs[0] + jnp.maximum(jnp.where(has_below, -side_total, nothing), 0.0)
@@ -270,7 +310,11 @@
         for u in range(2):
             d = i * 2 + u
             turn = cols - 1 - 2 * d
-            net[d] = net[d] + jnp.where(edge, pltpu.roll(colflow[0], turn, 1), 0.0)
+            flow = net[d] + jnp.where(edge, pltpu.roll(colflow[0], turn, 1), 0.0)
+            net[d] = flow
+            at = pl.multiple_of(d * brick_rows, brick_rows)
+            for p in range(n_wide):
+                slab[p, pl.ds(at, brick_rows), :] = flow[p * brick_rows:(p + 1) * brick_rows]
             most = jnp.maximum(
                 most, outs[d] + jnp.where(edge, pltpu.roll(colflow[1], turn, 1), 0.0)
             )
@@ -281,17 +325,36 @@
     maxw[w] = jnp.max(most.reshape(rows // brick_rows, brick_rows, cols), axis=0)
     wait_wide = everyone("wide", lambda peer: maxw.at[w], lambda sender: maxw.at[sender])
 
+    def part(sender):
+        return netb.at[pl.ds(pl.multiple_of(sender * band, band), band), :]
+
+    bulk = count[0]
+
+    def brick_copy(number, sender, peer):
+        return remote(slab.at[peer], part(sender), bulk + number, "wide", peer)
+
+    for off in range(1, n_wide):
+        slot()
+        brick_copy(off - 1, w, lax.rem(w + off, n_wide)).start()
+    netb[pl.ds(pl.multiple_of(w * band, band), band), :] = slab[w]
+
     all_cols = cols * n_narrow
     for copy in loading[4:]:
         copy.wait()
     cell = row * cols + lane
 
+    def split(column):
+        if all_cols & (all_cols - 1):
+            return lax.div(column, all_cols), lax.rem(column, all_cols)
+        return column >> (all_cols.bit_length() - 1), column & (all_cols - 1)
+
     def well(i, total):
         for u in range(8):
-            column = wcol_ref[i * 8 + u]
-            inside = lax.rem(column, all_cols) - k * cols
-            target = lax.div(column, all_cols) * cols + inside
-            target = jnp.where((inside >= 0) & (inside < cols), target, -1)
+            well_row, well_col = split(wcol_ref[i * 8 + u])
+            inside = well_col - k * cols
+            target = jnp.where(
+                (inside >= 0) & (inside < cols), well_row * cols + inside, -1
+            )
             total = total + jnp.where(cell == target, wrate_ref[i * 8 + u], 0.0)
         return total
 
@@ -301,66 +364,39 @@
         return total + jnp.sum(res_ref[pl.ds(i * 16, 16)], axis=0)
 
     res_total = jnp.sum(lax.fori_loop(0, layers // 16, add_res, zero), axis=(0, 1), keepdims=True)
+
+    def at_layer(z):
+        return pl.ds(pl.multiple_of(z * brick_rows, brick_rows), brick_rows)
+
+    def look_up_band(band_number):
+        for u in range(depth):
+            z = band_number * depth + u
+            perm, water, oil = properties(rockb[z])
+            coef[at_layer(z), :] = perm
+            rface[at_layer(z), :] = water
+            cface[at_layer(z), :] = oil
+
+    for copy in own_raw:
+        copy.wait()
+    look_up_band(w)
+
+    def take_raw(off, carry):
+        sender = lax.rem(w + n_wide - off, n_wide)
+        for f in range(2):
+            raw_copy(off, f, sender, sender).wait_recv()
+        look_up_band(sender)
+        return carry
+
+    lax.fori_loop(1, n_wide, take_raw, 0)
+
     wait_wide()
     maxn[k] = jnp.max(maxw[...], axis=0)
     everyone("narrow", lambda peer: maxn.at[k], lambda sender: maxn.at[sender])()
     top_rate = jnp.max(jnp.max(maxn[...], axis=0), axis=(0, 1), keepdims=True)
     step_size = courant / (top_rate + tiny)
 
-    def update(i, carry):
-        for u in range(2):
-            d = i * 2 + u
-            s = sat_ref[d] - step_size * net[d] + step_size * source[...]
-            satnew_ref[d] = s
-            value = fields[d + 1, 1] * (gains[d, 0] * s * s + gains[d, 1] * (1.0 - s) * (1.0 - s))
-            at = pl.multiple_of(d * brick_rows, brick_rows)
-            for p in range(n_wide):
-                slab[p, pl.ds(at, brick_rows), :] = value[p * brick_rows:(p + 1) * brick_rows]
-        return carry
-
-    lax.fori_loop(0, depth // 2, update, 0)
-
-    def part(sender):
-        return coef.at[pl.ds(pl.multiple_of(sender * band, band), band), :]
-
-    bulk = count[0]
-
-    def brick_copy(number, sender, peer):
-        return remote(slab.at[peer], part(sender), bulk + number, "wide", peer)
-
-    for off in range(1, n_wide):
-        slot()
-        brick_copy(off - 1, w, lax.rem(w + off, n_wide)).start()
-    storing = pltpu.make_async_copy(satnew_ref, satnew_out, loads.at[0])
-    storing.start()
-
-    def survey(i, carry):
-        total, cross, packed_low, packed_high = carry
-        for u in range(2):
-            d = i * 2 + u
-            at = pl.ds(pl.multiple_of(d * brick_rows, brick_rows), brick_rows)
-            value = jnp.concatenate([slab[p, at, :] for p in range(n_wide)], axis=0)
-            turned = pltpu.roll(value, d, 1)
-            packed_low = jnp.where(lane == d, turned, packed_low)
-            packed_high = jnp.where(lane == lax.rem(d + cols - 1, cols), turned, packed_high)
-            cross = cross + harmonic(value, pltpu.roll(value, rows - 1, 0))
-            total = total + value
-        return total, cross, packed_low, packed_high
-
-    total, cross, packed_low, packed_high = lax.fori_loop(
-        0, depth // 2, survey, (nothing, nothing, blank, blank)
-    )
-    sidepack[0] = packed_low
-    sidepack[1] = pltpu.roll(packed_high, 1, 1)
-    wait_sides = neighbours(
-        "narrow", sidepack.at[0], sidepack.at[1], sidehalo.at[0], sidehalo.at[1]
-    )
-
     last_row = brick_rows - 1
     packs[...] = jnp.zeros(packs.shape, F32)
-
-    def at_layer(z):
-        return pl.ds(pl.multiple_of(z * brick_rows, brick_rows), brick_rows)
 
     def assemble_band(band_number):
         base = band_number * depth
@@ -368,13 +404,17 @@
         tile = at_layer(lax.div(base, cols))
         low = packs[0, 0, tile, :]
         high = packs[1, 0, tile, :]
+        wells = step_size * source[pl.ds(pl.multiple_of(w * brick_rows, brick_rows), brick_rows), :]
         for u in range(depth):
-            here = coef[at_layer(base + u), :]
+            at = at_layer(base + u)
+            s = satb[base + u] - step_size * netb[at, :] + wells
+            here = coef[at, :] * (rface[at, :] * s * s + cface[at, :] * (1.0 - s) * (1.0 - s))
+            coef[at, :] = here
             rf = jnp.where(trow == last_row, 0.0, harmonic(here, pltpu.roll(here, last_row, 0)))
             cf = jnp.where(tlane == cols - 1, 0.0, harmonic(here, pltpu.roll(here, cols - 1, 1)))
-            rface[at_layer(base + u), :] = rf
-            cface[at_layer(base + u), :] = cf
-            scale[at_layer(base + u), :] = (
+            rface[at, :] = rf
+            cface[at, :] = cf
+            scale[at, :] = (
                 compress * here + pltpu.roll(rf, 1, 0) + rf + pltpu.roll(cf, 1, 1) + cf
             )
             spot = lane_base + u
@@ -384,31 +424,7 @@
         packs[0, 0, tile, :] = low
         packs[1, 0, tile, :] = high
 
-    coef[pl.ds(pl.multiple_of(w * band, band), band), :] = slab[w]
     assemble_band(w)
-
-    brick_count = n_wide
-
-    def by_brick(block):
-        summed = jnp.sum(block.reshape(brick_count, brick_rows, cols), axis=1)
-        return jnp.sum(summed, axis=1, keepdims=True)
-
-    clane = lax.broadcasted_iota(jnp.int32, (brick_count, cols), 1)
-    crow = lax.broadcasted_iota(jnp.int32, (brick_count, cols), 0)
-    high_rows = by_brick(jnp.where((lax.rem(row, brick_rows) == brick_rows - 1) & (row < rows - 1), cross, 0.0))
-    low_rows = by_brick(
-        pltpu.roll(jnp.where((lax.rem(row, brick_rows) == brick_rows - 1) & (row < rows - 1), cross, 0.0), 1, 0)
-    )
-    coef_sum = by_brick(total)
-    wait_sides()
-    low_cols = by_brick(jnp.where((lane < depth) & has_left, harmonic(sidepack[0], sidehalo[0]), 0.0))
-    high_cols = by_brick(jnp.where((lane < depth) & has_right, harmonic(sidepack[1], sidehalo[1]), 0.0))
-    diagonal = compress * coef_sum + low_rows + high_rows + low_cols + high_cols
-    message = jnp.where((clane == 0) & (crow == w), res_total, 0.0)
-    for i, value in enumerate((diagonal, low_rows, high_rows, low_cols, high_cols)):
-        message = jnp.where(clane == i + 1, value, message)
-    cw[w] = message
-    wait_sums = everyone("wide", lambda peer: cw.at[w], lambda sender: cw.at[sender])
 
     def take_band(off, carry):
         sender = lax.rem(w + n_wide - off, n_wide)
@@ -417,15 +433,66 @@
         return carry
 
     lax.fori_loop(1, n_wide, take_band, 0)
-    wait_sums()
+
+    def update(i, carry):
+        total, cross, packed_low, packed_high = carry
+        for u in range(2):
+            d = i * 2 + u
+            s = sat_ref[d] - step_size * net[d] + step_size * source[...]
+            satnew_ref[d] = s
+            value = fields[d + 1, 1] * (gains[d, 0] * s * s + gains[d, 1] * (1.0 - s) * (1.0 - s))
+            turned = pltpu.roll(value, d, 1)
+            packed_low = jnp.where(lane == d, turned, packed_low)
+            packed_high = jnp.where(lane == lax.rem(d + cols - 1, cols), turned, packed_high)
+            cross = cross + harmonic(value, pltpu.roll(value, rows - 1, 0))
+            total = total + value
+        return total, cross, packed_low, packed_high
+
+    total, cross, packed_low, packed_high = lax.fori_loop(
+        0, depth // 2, update, (nothing, nothing, blank, blank)
+    )
+    sidepack[0] = packed_low
+    sidepack[1] = pltpu.roll(packed_high, 1, 1)
+    wait_sides = neighbours(
+        "narrow", sidepack.at[0], sidepack.at[1], sidehalo.at[0], sidehalo.at[1]
+    )
+    storing = pltpu.make_async_copy(satnew_ref, satnew_out, loads.at[0])
+    storing.start()
+
+    def by_brick(block):
+        summed = jnp.sum(block.reshape(n_wide, brick_rows, cols), axis=1)
+        return jnp.sum(summed, axis=1, keepdims=True)
+
+    clane = lax.broadcasted_iota(jnp.int32, (n_wide, cols), 1)
+    crow = lax.broadcasted_iota(jnp.int32, (n_wide, cols), 0)
+
+    def send_sums():
+        crossing = jnp.where(
+            (lax.rem(row, brick_rows) == last_row) & (row < rows - 1), cross, 0.0
+        )
+        high_rows = by_brick(crossing)
+        low_rows = by_brick(pltpu.roll(crossing, 1, 0))
+        coef_sum = by_brick(total)
+        wait_sides()
+        low_cols = by_brick(
+            jnp.where((lane < depth) & has_left, harmonic(sidepack[0], sidehalo[0]), 0.0)
+        )
+        high_cols = by_brick(
+            jnp.where((lane < depth) & has_right, harmonic(sidepack[1], sidehalo[1]), 0.0)
+        )
+        diagonal = compress * coef_sum + low_rows + high_rows + low_cols + high_cols
+        message = jnp.where((clane == 0) & (crow == w), res_total, 0.0)
+        for i, value in enumerate((diagonal, low_rows, high_rows, low_cols, high_cols)):
+            message = jnp.where(clane == i + 1, value, message)
+        cw[w] = message
+        return everyone("wide", lambda peer: cw.at[w], lambda sender: cw.at[sender])
 
     def at_narrow(sender):
         return cn.at[pl.ds(pl.multiple_of(sender * n_wide, n_wide), n_wide), :]
 
-    cn[pl.ds(pl.multiple_of(k * n_wide, n_wide), n_wide), :] = jnp.sum(cw[...], axis=0)
-    wait_coarse = everyone("narrow", lambda peer: at_narrow(k), at_narrow)
-    for off in range(1, n_wide):
-        brick_copy(off - 1, w, lax.rem(w + off, n_wide)).wait_send()
+    def send_rows():
+        cn[pl.ds(pl.multiple_of(k * n_wide, n_wide), n_wide), :] = jnp.sum(cw[...], axis=0)
+        return everyone("narrow", lambda peer: at_narrow(k), at_narrow)
 
     def send_sides(ref, which):
         rowsend[0, which] = ref[pl.ds(0, layers, stride=brick_rows), :]
@@ -532,7 +599,12 @@
         sweep(False)
         return carry
 
-    lax.fori_loop(0, SWEEPS - 2, plain_sweep, 0)
+    wait_sums = send_sums()
+    early = (SWEEPS - 2) // 2
+    lax.fori_loop(0, early, plain_sweep, 0)
+    wait_sums()
+    wait_coarse = send_rows()
+    lax.fori_loop(early, SWEEPS - 2, plain_sweep, 0)
     sweep(True)
     wait_value_rows, wait_value_packs = send_sides(va, 1)
     wait_coarse()
@@ -581,6 +653,11 @@
 
         lax.fori_loop(0, cols // unroll, average, 0)
 
+    for off in range(1, n_wide):
+        peer = lax.rem(w + off, n_wide)
+        for f in range(2):
+            raw_copy(off, f, w, peer).wait_send()
+        brick_copy(off - 1, w, peer).wait_send()
     storing.wait()
     for i in range(layers // unroll):
         store(i).wait()
@@ -610,7 +687,7 @@
     tiles = layers // cols
     bricks = n_wide * n_narrow
     cells = layers * brick_rows
-    copies = 2 * 7 + 3 * (n_wide - 1) + 2 * (n_narrow - 1)
+    copies = 2 * 9 + 5 * (n_wide - 1) + 2 * (n_narrow - 1)
     anywhere = pl.BlockSpec(memory_space=pl.ANY)
     table, wells = args[3].shape, args[4].shape
 
@@ -663,7 +740,13 @@
             buffer(bricks, cols),
             buffer(2, rows, cols),
             buffer(2, rows, cols),
-            pltpu.SemaphoreType.DMA((7,)),
+            buffer(2, rows, cols),
+            buffer(2, rows, cols),
+            pltpu.VMEM((2, rows, cols), jnp.int32),
+            buffer(*residual.shape),
+            pltpu.VMEM(residual.shape, jnp.int32),
+            buffer(cells, cols),
+            pltpu.SemaphoreType.DMA((9,)),
             pltpu.SemaphoreType.DMA((layers // 32,)),
             pltpu.SemaphoreType.DMA((copies,)),
             pltpu.SemaphoreType.DMA((copies,)),

time: 38.8 us -> 45.6 us (1.18)
  Pallas kernels: 38 us -> 44.7 us
    pallas_call x1, Pallas kernels: 36 us -> 42.6 us  [shards(): pl.pallas_call(functools.partial(kernel, n_wide, n_narrow), out_shape=(ja...]
where the time goes in v6:
time: 45.6 us; the launch traced here: 45.3 us
  Pallas kernels  44.7 us (98%)
  between operations  0.64 us (1%)
    pallas_call x1, Pallas kernels, shards(): pl.pallas_call(functools.partial(kernel, n_wide, n_narrow), out_shape=(ja...  42.6 us
    pallas_call x1, Pallas kernels, shards(): pl.pallas_call(deliver, out_shape=(jax.ShapeDtypeStruct(sat.shape, F32),...  2.09 us

profile of v6, /device:TPU:1, one launch (start us, length us, event | category | flops | bytes accessed | tf_op | source)
XLA Modules:
  0.0 45.3 jit_solution(8659882107639210328)
XLA Ops:
  0.6 42.6 %shard_map.86 = (f32[16,64,128]{2,1,0:T(8,128)}, f32[128,8,128]{2,1,0:T(8,128)}) custom-call(f32[16,64,128]{2,1,0:T(8,128)} %sat_in.1, f32[16,64,128]{2,1,0:T(8,128)} %pres_in.1, s32[16,64,128]{2,1,0:T(8,128)} %rock_in.1, f32[3,16]{1,0:T(4,128)} %table_in.1, s32[64]{0:T(128)} %wcol_in.1, f32[64]{0:T(128)} %wrate_in.1, f32[128,8,128]{2,1,0:T(8,128)} %res_in.1), custom_call_target="tpu_custom_call" | custom-call | tf_op jit(solution)/shard_map/pallas_call | solution.py:697
  43.3 2.1 %shard_map.87 = (f32[16,64,128]{2,1,0:T(8,128)}, f32[128,8,128]{2,1,0:T(8,128)}) custom-call(f32[16,64,128]{2,1,0:T(8,128)} %get-tuple-element.4.a_in, f32[128,8,128]{2,1,0:T(8,128)} %get-tuple-element.5.b_in), custom_call_target="tpu_custom_call" | custom-call | tf_op jit(solution)/shard_map/pallas_call | solution.py:758

commit v7 on v5

--- a/solution.py
+++ b/solution.py
@@ -43,6 +43,7 @@
     fields, gains, net, colpack, colhalo, colflow, source, maxw, maxn,
     slab, coef, dface, rface, cface, scale, first, va,
     rowsend, rowhalo, rowterm, packs, packhalo, packterm, cw, cn, sidepack, sidehalo,
+    satb, rockb, netb, netslab,
     loads, stores, sends, recvs,
 ):
     depth, rows, cols = sat_ref.shape
@@ -129,6 +130,20 @@
 
         return wait
 
+    def xor(a, b):
+        total, bit = 0, 1
+        while bit < n_wide:
+            total = total + bit * lax.rem(lax.div(a, bit) + lax.div(b, bit), 2)
+            bit *= 2
+        return total
+
+    odd = lax.rem(w, 2)
+    order = list(range(2, n_wide, 2)) + list(range(3, n_wide, 2)) + [1]
+    distances = []
+    for off in order:
+        other = off ^ 6 if n_wide >= 8 and off in (2, 3, 4, 5) else off
+        distances.append(off + odd * (other - off))
+
     lane = lax.broadcasted_iota(jnp.int32, (rows, cols), 1)
     row = lax.broadcasted_iota(jnp.int32, (rows, cols), 0)
     tlane = lax.broadcasted_iota(jnp.int32, (brick_rows, cols), 1)
@@ -165,17 +180,17 @@
     for copy in loading[:4]:
         copy.wait()
 
-    def derive(d, carry):
-        packed_low, packed_high = carry
-        rock = rock_ref[d]
+    def properties(rock):
         bits = []
         step = 1
         while step < rocks:
             bits.append((rock & step) != 0)
             step *= 2
-        perm = lookup(bits, table_ref, 0, rocks)
-        water = lookup(bits, table_ref, 1, rocks)
-        oil = lookup(bits, table_ref, 2, rocks)
+        return [lookup(bits, table_ref, i, rocks) for i in range(3)]
+
+    def derive(d, carry):
+        packed_low, packed_high = carry
+        perm, water, oil = properties(rock_ref[d])
         s = sat_ref[d]
         water_mob = water * s * s
         oil_mob = oil * (1.0 - s) * (1.0 - s)
@@ -203,6 +218,37 @@
         "narrow", colpack.at[0], colpack.at[1], colhalo.at[0], colhalo.at[1]
     )
 
+    ahead = depth // 4
+
+    def brick_part(ref, sender):
+        return ref.at[pl.ds(sender * ahead, ahead)]
+
+    def brick_rows_of(ref, peer):
+        return ref.at[
+            pl.ds(0, ahead), pl.ds(pl.multiple_of(peer * brick_rows, brick_rows), brick_rows), :
+        ]
+
+    raw = count[0]
+    raw_fields = ((sat_ref, satb), (rock_ref, rockb))
+
+    def raw_copy(distance, f, sender, peer):
+        src, dst = raw_fields[f]
+        return remote(
+            brick_rows_of(src, peer), brick_part(dst, sender),
+            raw + 2 * (distance - 1) + f, "wide", peer,
+        )
+
+    for distance in distances:
+        for f in range(2):
+            slot()
+            raw_copy(distance, f, w, xor(w, distance)).start()
+    own_raw = [
+        pltpu.make_async_copy(brick_rows_of(src, w), brick_part(dst, w), loads.at[7 + f])
+        for f, (src, dst) in enumerate(raw_fields)
+    ]
+    for copy in own_raw:
+        copy.start()
+
     nothing = jnp.zeros((rows, cols), F32)
     has_below, has_above = has["wide"]
     has_left, has_right = has["narrow"]
@@ -280,18 +326,45 @@
 
     maxw[w] = jnp.max(most.reshape(rows // brick_rows, brick_rows, cols), axis=0)
     wait_wide = everyone("wide", lambda peer: maxw.at[w], lambda sender: maxw.at[sender])
+    ahead_rows = ahead * brick_rows
+    for d in range(ahead):
+        for p in range(n_wide):
+            netslab[p, pl.ds(d * brick_rows, brick_rows), :] = net[
+                d, pl.ds(p * brick_rows, brick_rows), :
+            ]
+
+    def net_part(sender):
+        return netb.at[pl.ds(pl.multiple_of(sender * ahead_rows, ahead_rows), ahead_rows), :]
+
+    net_base = count[0]
+
+    def net_copy(distance, sender, peer):
+        return remote(
+            netslab.at[peer], net_part(sender), net_base + distance - 1, "wide", peer
+        )
+
+    for distance in distances:
+        slot()
+        net_copy(distance, w, xor(w, distance)).start()
+    netb[pl.ds(pl.multiple_of(w * ahead_rows, ahead_rows), ahead_rows), :] = netslab[w]
 
     all_cols = cols * n_narrow
     for copy in loading[4:]:
         copy.wait()
     cell = row * cols + lane
 
+    def split(column):
+        if all_cols & (all_cols - 1):
+            return lax.div(column, all_cols), lax.rem(column, all_cols)
+        return column >> (all_cols.bit_length() - 1), column & (all_cols - 1)
+
     def well(i, total):
         for u in range(8):
-            column = wcol_ref[i * 8 + u]
-            inside = lax.rem(column, all_cols) - k * cols
-            target = lax.div(column, all_cols) * cols + inside
-            target = jnp.where((inside >= 0) & (inside < cols), target, -1)
+            well_row, well_col = split(wcol_ref[i * 8 + u])
+            inside = well_col - k * cols
+            target = jnp.where(
+                (inside >= 0) & (inside < cols), well_row * cols + inside, -1
+            )
             total = total + jnp.where(cell == target, wrate_ref[i * 8 + u], 0.0)
         return total
 
@@ -301,6 +374,30 @@
         return total + jnp.sum(res_ref[pl.ds(i * 16, 16)], axis=0)
 
     res_total = jnp.sum(lax.fori_loop(0, layers // 16, add_res, zero), axis=(0, 1), keepdims=True)
+
+    def at_layer(z):
+        return pl.ds(pl.multiple_of(z * brick_rows, brick_rows), brick_rows)
+
+    def look_up_band(band_number):
+        for u in range(ahead):
+            at = at_layer(band_number * depth + u)
+            perm, water, oil = properties(rockb[band_number * ahead + u])
+            coef[at, :] = perm
+            rface[at, :] = water
+            cface[at, :] = oil
+
+    for copy in own_raw:
+        copy.wait()
+    look_up_band(w)
+
+    def take_raw(distance, carry):
+        sender = xor(w, distance)
+        for f in range(2):
+            raw_copy(distance, f, sender, sender).wait_recv()
+        look_up_band(sender)
+        return carry
+
+    lax.fori_loop(1, n_wide, take_raw, 0)
     wait_wide()
     maxn[k] = jnp.max(maxw[...], axis=0)
     everyone("narrow", lambda peer: maxn.at[k], lambda sender: maxn.at[sender])()
@@ -320,17 +417,24 @@
 
     lax.fori_loop(0, depth // 2, update, 0)
 
+    late_rows = band - ahead_rows
+
     def part(sender):
-        return coef.at[pl.ds(pl.multiple_of(sender * band, band), band), :]
+        return coef.at[
+            pl.ds(pl.multiple_of(sender * band + ahead_rows, brick_rows), late_rows), :
+        ]
 
     bulk = count[0]
 
-    def brick_copy(number, sender, peer):
-        return remote(slab.at[peer], part(sender), bulk + number, "wide", peer)
-
-    for off in range(1, n_wide):
+    def brick_copy(distance, sender, peer):
+        return remote(
+            slab.at[peer, pl.ds(ahead_rows, late_rows), :], part(sender),
+            bulk + distance - 1, "wide", peer,
+        )
+
+    for distance in distances:
         slot()
-        brick_copy(off - 1, w, lax.rem(w + off, n_wide)).start()
+        brick_copy(distance, w, xor(w, distance)).start()
     storing = pltpu.make_async_copy(satnew_ref, satnew_out, loads.at[0])
     storing.start()
 
@@ -359,17 +463,21 @@
     last_row = brick_rows - 1
     packs[...] = jnp.zeros(packs.shape, F32)
 
-    def at_layer(z):
-        return pl.ds(pl.multiple_of(z * brick_rows, brick_rows), brick_rows)
-
     def assemble_band(band_number):
         base = band_number * depth
         lane_base = lax.rem(base, cols)
         tile = at_layer(lax.div(base, cols))
         low = packs[0, 0, tile, :]
         high = packs[1, 0, tile, :]
+        own_wells = step_size * source[at_layer(w), :]
         for u in range(depth):
             here = coef[at_layer(base + u), :]
+            if u < ahead:
+                at = at_layer(base + u)
+                near = band_number * ahead + u
+                s = satb[near] - step_size * netb[at_layer(near), :] + own_wells
+                here = here * (rface[at, :] * s * s + cface[at, :] * (1.0 - s) * (1.0 - s))
+                coef[at, :] = here
             rf = jnp.where(trow == last_row, 0.0, harmonic(here, pltpu.roll(here, last_row, 0)))
             cf = jnp.where(tlane == cols - 1, 0.0, harmonic(here, pltpu.roll(here, cols - 1, 1)))
             rface[at_layer(base + u), :] = rf
@@ -384,7 +492,9 @@
         packs[0, 0, tile, :] = low
         packs[1, 0, tile, :] = high
 
-    coef[pl.ds(pl.multiple_of(w * band, band), band), :] = slab[w]
+    coef[pl.ds(pl.multiple_of(w * band + ahead_rows, brick_rows), late_rows), :] = slab[
+        w, pl.ds(ahead_rows, late_rows), :
+    ]
     assemble_band(w)
 
     brick_count = n_wide
@@ -410,9 +520,10 @@
     cw[w] = message
     wait_sums = everyone("wide", lambda peer: cw.at[w], lambda sender: cw.at[sender])
 
-    def take_band(off, carry):
-        sender = lax.rem(w + n_wide - off, n_wide)
-        brick_copy(off - 1, sender, sender).wait_recv()
+    def take_band(distance, carry):
+        sender = xor(w, distance)
+        net_copy(distance, sender, sender).wait_recv()
+        brick_copy(distance, sender, sender).wait_recv()
         assemble_band(sender)
         return carry
 
@@ -424,8 +535,6 @@
 
     cn[pl.ds(pl.multiple_of(k * n_wide, n_wide), n_wide), :] = jnp.sum(cw[...], axis=0)
     wait_coarse = everyone("narrow", lambda peer: at_narrow(k), at_narrow)
-    for off in range(1, n_wide):
-        brick_copy(off - 1, w, lax.rem(w + off, n_wide)).wait_send()
 
     def send_sides(ref, which):
         rowsend[0, which] = ref[pl.ds(0, layers, stride=brick_rows), :]
@@ -581,6 +690,12 @@
 
         lax.fori_loop(0, cols // unroll, average, 0)
 
+    for distance in range(1, n_wide):
+        peer = xor(w, distance)
+        for f in range(2):
+            raw_copy(distance, f, w, peer).wait_send()
+        net_copy(distance, w, peer).wait_send()
+        brick_copy(distance, w, peer).wait_send()
     storing.wait()
     for i in range(layers // unroll):
         store(i).wait()
@@ -610,7 +725,8 @@
     tiles = layers // cols
     bricks = n_wide * n_narrow
     cells = layers * brick_rows
-    copies = 2 * 7 + 3 * (n_wide - 1) + 2 * (n_narrow - 1)
+    ahead = depth // 4
+    copies = 2 * 7 + 6 * (n_wide - 1) + 2 * (n_narrow - 1)
     anywhere = pl.BlockSpec(memory_space=pl.ANY)
     table, wells = args[3].shape, args[4].shape
 
@@ -663,7 +779,11 @@
             buffer(bricks, cols),
             buffer(2, rows, cols),
             buffer(2, rows, cols),
-            pltpu.SemaphoreType.DMA((7,)),
+            buffer(n_wide * ahead, brick_rows, cols),
+            pltpu.VMEM((n_wide * ahead, brick_rows, cols), jnp.int32),
+            buffer(n_wide * ahead * brick_rows, cols),
+            buffer(n_wide, ahead * brick_rows, cols),
+            pltpu.SemaphoreType.DMA((9,)),
             pltpu.SemaphoreType.DMA((layers // 32,)),
             pltpu.SemaphoreType.DMA((copies,)),
             pltpu.SemaphoreType.DMA((copies,)),

time: 38.8 us -> 39.5 us (1.018)
  Pallas kernels: 38 us -> 38.4 us
where the time goes in v7:
time: 39.5 us; the launch traced here: 39 us
  Pallas kernels  38.4 us (97%)
  between operations  0.64 us (2%)
    pallas_call x1, Pallas kernels, shards(): pl.pallas_call(functools.partial(kernel, n_wide, n_narrow), out_shape=(ja...  36.3 us
    pallas_call x1, Pallas kernels, shards(): pl.pallas_call(deliver, out_shape=(jax.ShapeDtypeStruct(sat.shape, F32),...  2.09 us

profile of v7, /device:TPU:1, one launch (start us, length us, event | category | flops | bytes accessed | tf_op | source)
XLA Modules:
  0.0 39.0 jit_solution(16474206755201235891)
XLA Ops:
  0.6 36.3 %shard_map.86 = (f32[16,64,128]{2,1,0:T(8,128)}, f32[128,8,128]{2,1,0:T(8,128)}) custom-call(f32[16,64,128]{2,1,0:T(8,128)} %sat_in.1, f32[16,64,128]{2,1,0:T(8,128)} %pres_in.1, s32[16,64,128]{2,1,0:T(8,128)} %rock_in.1, f32[3,16]{1,0:T(4,128)} %table_in.1, s32[64]{0:T(128)} %wcol_in.1, f32[64]{0:T(128)} %wrate_in.1, f32[128,8,128]{2,1,0:T(8,128)} %res_in.1), custom_call_target="tpu_custom_call" | custom-call | tf_op jit(solution)/shard_map/pallas_call | solution.py:736
  37.0 2.1 %shard_map.87 = (f32[16,64,128]{2,1,0:T(8,128)}, f32[128,8,128]{2,1,0:T(8,128)}) custom-call(f32[16,64,128]{2,1,0:T(8,128)} %get-tuple-element.4.a_in, f32[128,8,128]{2,1,0:T(8,128)} %get-tuple-element.5.b_in), custom_call_target="tpu_custom_call" | custom-call | tf_op jit(solution)/shard_map/pallas_call | solution.py:795
